TPU v7x, 256 devices: a whole 4x4x8 slice. The times are simulated.
256 devices in a mesh: seq: 32 (over y, x, core), head: 8 (over z).
Axes of the slice: x: 4, y: 4, z: 8, core: 2. Of those that a mesh axis runs over, the one named last changes fastest.
Arguments:
- queries: bfloat16 [6144, 2048], P('seq', 'head'), may hold values from -6 to 6
- key_states: bfloat16 [6144, 2048], P('seq', 'head'), may hold values from -6 to 6
- value_states: bfloat16 [6144, 2048], P('seq', 'head'), may hold values from -6 to 6
- w_out: bfloat16 [2048, 4096], P('head'), may hold values from -0.125 to 0.125
- grad_y: bfloat16 [6144, 4096], P('seq'), may hold values from -6 to 6
- chain_order: int32 [32], replicated, may hold values from 0 to 31, each once
Outputs:
- layer_out: bfloat16 [6144, 4096], P('seq', 'head')
- grad_queries: bfloat16 [6144, 2048], P('seq', 'head')
- grad_keys: bfloat16 [6144, 2048], P('seq', 'head')
- grad_values: bfloat16 [6144, 2048], P('seq', 'head')
- grad_weight: bfloat16 [2048, 4096], P('head', 'seq')
Inputs may be any that keep to these rules, and one draw needn't show every extreme that they name: chain_order names each of 0 to 31 once.
All inputs are finite; a program needn't handle non-finite values.
Results may differ from a plain program's by a relative error of at most 0.025.
Values may be sent and summed in bfloat16 or wider, within the bound.
A program may use at most 64 MiB of HBM per device.

v0:
```python
import math

import jax
import jax.numpy as jnp
from jax import lax
from jax.sharding import PartitionSpec as P

HEAD_DIM = 128


neg_big = -1e30


def tile_size(row_count):
    tile_rows = min(row_count, 512)
    while row_count % tile_rows:
        tile_rows -= 1
    return tile_rows


def chain_positions(chain_order, global_rows, shard_rows):
    block_index = global_rows // shard_rows
    numbers = jnp.arange(chain_order.shape[0], dtype=jnp.int32)
    owner_block = jnp.sum(
        jnp.where(block_index[:, None] == numbers[None, :], chain_order[None, :], 0), axis=1
    )
    return owner_block * shard_rows + global_rows % shard_rows


def split_heads(matrix, head_count):
    return matrix.reshape(matrix.shape[0], head_count, -1)


def over_tiles(update, carried, members):
    row_count = members[0].shape[0]
    tile_rows = tile_size(row_count)
    stacked = tuple(
        (
            member.reshape((row_count // tile_rows, tile_rows) + member.shape[1:])
            for member in members
        )
    )
    offsets = tile_rows * jnp.arange(row_count // tile_rows, dtype=jnp.int32)

    def advance(running_state, scanned):
        return (update(running_state, scanned[0], scanned[1]), None)

    result, unused = lax.scan(advance, carried, (stacked, offsets))
    return result


def shards(queries, key_states, value_states, w_out, grad_y, chain_order):
    shard_rows = queries.shape[0]
    head_count = w_out.shape[0] // HEAD_DIM
    score_scale = 1.0 / math.sqrt(HEAD_DIM)
    chain_index = lax.axis_index("seq")
    own_rows = chain_index * shard_rows + jnp.arange(shard_rows, dtype=jnp.int32)
    own_pos = chain_positions(chain_order, own_rows, shard_rows)
    q_heads = split_heads(queries, head_count)
    k_heads = split_heads(key_states, head_count)
    v_heads = split_heads(value_states, head_count)

    def forward_update(running_state, tile, first_row):
        key_tile, value_tile = tile
        key_pos = chain_positions(
            chain_order, first_row + jnp.arange(key_tile.shape[0], dtype=jnp.int32), shard_rows
        )
        running, denominator, accumulated = running_state
        scores = (
            jnp.einsum(
                "qhd,khd->hqk",
                q_heads,
                split_heads(key_tile, head_count),
                preferred_element_type=jnp.float32,
            )
            * score_scale
        )
        allowed = key_pos[None, :] <= own_pos[:, None]
        scores = jnp.where(allowed[None], scores, -jnp.inf)
        raised = jnp.maximum(running, jnp.max(scores, axis=2))
        factor = jnp.exp(running - raised)
        weights = jnp.exp(scores - raised[:, :, None])
        denominator = denominator * factor + jnp.sum(weights, axis=2)
        accumulated = accumulated * factor[:, :, None] + jnp.einsum(
            "hqk,khd->hqd",
            weights.astype(jnp.bfloat16),
            split_heads(value_tile, head_count),
            preferred_element_type=jnp.float32,
        )
        return (raised, denominator, accumulated)

    zeros_rows = jnp.zeros((head_count, shard_rows), jnp.float32)
    zeros_heads = jnp.zeros((head_count, shard_rows, HEAD_DIM), jnp.float32)
    forward_init = (
        jnp.full((head_count, shard_rows), neg_big, jnp.float32),
        zeros_rows,
        zeros_heads,
    )
    forward_state = over_tiles(
        forward_update,
        forward_init,
        (
            lax.all_gather(key_states, "seq", axis=0, tiled=True),
            lax.all_gather(value_states, "seq", axis=0, tiled=True),
        ),
    )
    running, denominator, accumulated = forward_state
    log_norm = running + jnp.log(denominator)
    attention = (accumulated / denominator[:, :, None]).astype(jnp.bfloat16)
    attention_rows = jnp.transpose(attention, (1, 0, 2)).reshape(shard_rows, -1)
    partial_out = jnp.dot(attention_rows, w_out, preferred_element_type=jnp.float32)
    layer_out = lax.psum_scatter(
        partial_out.astype(jnp.bfloat16), "head", scatter_dimension=1, tiled=True
    )
    grad_attention = lax.dot_general(
        grad_y, w_out, (((1,), (1,)), ((), ())), preferred_element_type=jnp.float32
    ).astype(jnp.bfloat16)
    weight_share = lax.psum_scatter(
        lax.dot_general(
            grad_y, attention_rows, (((0,), (0,)), ((), ())), preferred_element_type=jnp.float32
        ),
        "seq",
        scatter_dimension=0,
        tiled=True,
    )
    grad_weight = weight_share.T.astype(jnp.bfloat16)
    d_heads = split_heads(grad_attention, head_count)
    delta = jnp.sum(
        d_heads.astype(jnp.float32) * jnp.transpose(attention, (1, 0, 2)).astype(jnp.float32),
        axis=2,
    )
    delta_heads = delta.T
    log_rows = log_norm.T

    def query_update(accumulated_grad, tile, first_row):
        key_tile, value_tile = tile
        key_pos = chain_positions(
            chain_order, first_row + jnp.arange(key_tile.shape[0], dtype=jnp.int32), shard_rows
        )
        key_split = split_heads(key_tile, head_count)
        scores = (
            jnp.einsum("qhd,khd->hqk", q_heads, key_split, preferred_element_type=jnp.float32)
            * score_scale
        )
        allowed = key_pos[None, :] <= own_pos[:, None]
        scores = jnp.where(allowed[None], scores, -jnp.inf)
        probs = jnp.exp(scores - log_norm[:, :, None])
        slopes = jnp.einsum(
            "qhd,khd->hqk",
            d_heads,
            split_heads(value_tile, head_count),
            preferred_element_type=jnp.float32,
        )
        dscores = (probs * (slopes - delta_heads[:, :, None])).astype(jnp.bfloat16)
        return accumulated_grad + jnp.einsum(
            "hqk,khd->hqd", dscores, key_split, preferred_element_type=jnp.float32
        )

    query_grad = over_tiles(
        query_update,
        zeros_heads,
        (
            lax.all_gather(key_states, "seq", axis=0, tiled=True),
            lax.all_gather(value_states, "seq", axis=0, tiled=True),
        ),
    )

    def key_update(running_state, tile, first_row):
        query_wide, dout_wide, norm_tile, delta_tile = tile
        query_tile = query_wide.astype(jnp.bfloat16)
        dout_tile = dout_wide.astype(jnp.bfloat16)
        query_pos = chain_positions(
            chain_order, first_row + jnp.arange(query_tile.shape[0], dtype=jnp.int32), shard_rows
        )
        grad_k, grad_v = running_state
        query_split = split_heads(query_tile, head_count)
        dout_split = split_heads(dout_tile, head_count)
        scores = (
            jnp.einsum("qhd,khd->hqk", query_split, k_heads, preferred_element_type=jnp.float32)
            * score_scale
        )
        allowed = own_pos[None, :] <= query_pos[:, None]
        scores = jnp.where(allowed[None], scores, -jnp.inf)
        probs = jnp.exp(scores - norm_tile.T[:, :, None])
        grad_v = grad_v + jnp.einsum(
            "hqk,qhd->hkd",
            probs.astype(jnp.bfloat16),
            dout_split,
            preferred_element_type=jnp.float32,
        )
        slopes = jnp.einsum("qhd,khd->hqk", dout_split, v_heads, preferred_element_type=jnp.float32)
        dscores = (probs * (slopes - delta_tile.T[:, :, None])).astype(jnp.bfloat16)
        grad_k = grad_k + jnp.einsum(
            "hqk,qhd->hkd", dscores, query_split, preferred_element_type=jnp.float32
        )
        return (grad_k, grad_v)

    query_wide = queries.astype(jnp.float32)
    dout_wide = grad_attention.astype(jnp.float32)
    key_grad, value_grad = over_tiles(
        key_update,
        (zeros_heads, zeros_heads),
        (
            lax.all_gather(query_wide, "seq", axis=0, tiled=True),
            lax.all_gather(dout_wide, "seq", axis=0, tiled=True),
            lax.all_gather(log_rows, "seq", axis=0, tiled=True),
            lax.all_gather(delta, "seq", axis=0, tiled=True),
        ),
    )

    def merged(stacked):
        return jnp.transpose(stacked, (1, 0, 2)).reshape(shard_rows, -1).astype(jnp.bfloat16)

    return (
        layer_out,
        merged(query_grad * score_scale),
        merged(key_grad * score_scale),
        merged(value_grad),
        grad_weight,
    )


def solution(mesh):
    return jax.shard_map(
        shards,
        mesh=mesh,
        in_specs=(
            P("seq", "head"),
            P("seq", "head"),
            P("seq", "head"),
            P("head", None),
            P("seq", None),
            P(),
        ),
        out_specs=(
            P("seq", "head"),
            P("seq", "head"),
            P("seq", "head"),
            P("seq", "head"),
            P("head", "seq"),
        ),
        check_vma=False,
    )
```

profile of v0, /device:TPU:1, one launch (start us, length us, event | category | flops | bytes accessed | tf_op | source)
XLA Modules:
  0.0 439.5 jit_solution(5957514549231932933)
XLA Ops:
  9.5 2.9 convolution_convert_fusion.1
  15.6 49.3 %all-gather.7.cloned.1.call-done = bf16[6144,256]{1,0:T(8,128)(2,1)} async-done(((bf16[192,256]{1,0:T(8,128)(2,1)}), bf16[6144,256]{1,0:T(8,128)(2,1)}) %all-gather.7.cloned.1.call-update) | async-done | bytes 3145744 | tf_op jit(solution)/shard_map/all_gather | solution.py:103
  64.9 4.7 %copy.153 = bf16[12,512,256]{1,2,0:T(8,128)(2,1)} copy(bf16[12,512,256]{2,1,0:T(8,128)(2,1)} %bitcast.194) | data formatting | bytes 6291456
  69.6 47.4 %all-gather.9.cloned.1.call-done = bf16[6144,256]{1,0:T(8,128)(2,1)} async-done(((bf16[192,256]{1,0:T(8,128)(2,1)}), bf16[6144,256]{1,0:T(8,128)(2,1)}) %all-gather.9.cloned.1.call-update) | async-done | bytes 3145744 | tf_op jit(solution)/shard_map/all_gather | solution.py:104
  117.0 4.6 %copy.155 = bf16[12,512,256]{1,2,0:T(8,128)(2,1)} copy(bf16[12,512,256]{2,1,0:T(8,128)(2,1)} %bitcast.195) | data formatting | bytes 6291456
  121.6 51.2 %while.45 = (s32[]{:T(128)}, f32[2,192]{1,0:T(2,128)S(1)}, f32[2,192]{1,0:T(2,128)S(1)}, f32[2,192,128]{2,1,0:T(8,128)S(1)}, s32[12]{0:T(128)S(1)}, /*index=5*/s...) while((s32[]{:T(128)}, f32[2,192]{1,0:T(2,128)S(1)}, ...), condition=%wide.region_5.6_spmd.clone, body=%wide.region_1.5_spmd.clone.sunk | while | flops 102345088 | bytes 4658209 | solution.py:48
  172.8 23.5 %all-gather = f32[32,192,2]{1,2,0:T(2,128)S(1)} all-gather(f32[1,192,2]{1,2,0:T(2,128)S(1)} %bitcast.204), channel_id=1, replica_groups=mesh['seq'=32,'head'=8] {'seq'}, dimensions={0}, use_global_device_ids=true | all-gather | bytes 50688 | tf_op jit(solution)/shard_map/all_gather | solution.py:206
  198.2 22.2 %all-gather.1 = f32[32,192,2]{1,2,0:T(2,128)S(1)} all-gather(f32[1,192,2]{1,2,0:T(2,128)S(1)} %bitcast.200), channel_id=1, replica_groups=mesh['seq'=32,'head'=8] {'seq'}, dimensions={0}, use_global_device_ids=true | all-gather | bytes 50688 | tf_op jit(solution)/shard_map/all_gather | solution.py:207
  221.1 4.2 convolution_bitcast_fusion
  225.4 132.3 %while.47 = (s32[]{:T(128)}, f32[2,192,128]{2,1,0:T(8,128)}, f32[2,192,128]{2,1,0:T(8,128)}, s32[192]{0:T(256)S(1)}, s32[12]{0:T(128)S(1)}, /*index=5*/s32[32]{0...) while((s32[]{:T(128)}, f32[2,192,128]{2,1,0:T(8,128)}, ...), condition=%wide.region_13.14_spmd.clone, body=%wide.region_11.13_spmd.clone.sunk | while | flops 203055616 | bytes 6738996 | solution.py:48
  242.7 2.0 fusion.137
  253.9 2.0 fusion.137
  265.0 2.0 fusion.137
  276.1 2.1 fusion.137
  287.2 2.0 fusion.137
  298.3 2.0 fusion.137
  309.4 2.0 fusion.137
  320.5 2.0 fusion.137
  331.6 2.0 fusion.137
  342.7 2.0 fusion.137
  353.8 2.0 fusion.137
  357.7 2.7 convolution_convert_fusion
  360.4 66.8 %while.46 = (s32[]{:T(128)}, f32[2,192,128]{2,1,0:T(8,128)}, s32[12]{0:T(128)S(1)}, s32[32]{0:T(128)S(1)}, s32[192]{0:T(256)S(1)}, /*index=5*/bf16[12,512,256]{1...) while((s32[]{:T(128)}, f32[2,192,128]{2,1,0:T(8,128)}, ...), condition=%wide.region_10.11_spmd.clone, body=%wide.region_8.10_spmd.clone.sunk | while | flops 152429056 | bytes 4210727 | solution.py:48
  369.5 2.0 fusion.127
  375.0 2.0 fusion.127
  380.6 2.0 fusion.127
  386.2 2.0 fusion.127
  391.8 2.0 fusion.127
  397.3 2.0 fusion.127
  402.9 2.0 fusion.127
  408.5 2.0 fusion.127
  414.0 2.0 fusion.127
  (441 shorter events, 221.1 us)
Async XLA Ops:
  7.2 2.3 copy-start
  7.2 5.4 %copy-start.4 = (bf16[192,256]{1,0:T(8,128)(2,1)S(1)}, bf16[192,256]{1,0:T(8,128)(2,1)}, u32[]{:S(2)}) copy-start(bf16[192,256]{1,0:T(8,128)(2,1)} %param.12) | copy-start | bytes 294916
  7.2 57.7 %all-gather.7.cloned.1.call-start = ((), (), s32[]{:S(2)}) async-start(), calls=%async_computation.2 | async-start | bytes 3244032 | tf_op jit(solution)/shard_map/all_gather | solution.py:103
  7.9 109.1 %all-gather.9.cloned.1.call-start = ((), (), s32[]{:S(2)}) async-start(), calls=%async_computation.3 | async-start | bytes 3244032 | tf_op jit(solution)/shard_map/all_gather | solution.py:104
  8.7 216.7 %all-gather.11.cloned.1.call-start = ((), (), s32[]{:S(2)}) async-start(), calls=%async_computation.5 | async-start | bytes 3244032 | tf_op jit(solution)/shard_map/all_gather | solution.py:204
  9.4 4.7 %copy-start.2 = (bf16[192,256]{1,0:T(8,128)(2,1)S(1)}, bf16[192,256]{1,0:T(8,128)(2,1)}, u32[]{:S(2)}) copy-start(bf16[192,256]{1,0:T(8,128)(2,1)} %param.13) | copy-start | bytes 294916
  9.4 5.4 %copy-start.3 = (bf16[192,256]{1,0:T(8,128)(2,1)S(1)}, bf16[192,256]{1,0:T(8,128)(2,1)}, u32[]{:S(2)}) copy-start(bf16[192,256]{1,0:T(8,128)(2,1)} %param.14) | copy-start | bytes 294916
  9.4 6.0 %copy-start.5 = (s32[32]{0:T(128)S(1)}, s32[32]{0:T(128)}, u32[]{:S(2)}) copy-start(s32[32]{0:T(128)} %param.17) | copy-start | bytes 388
  9.4 216.0 %all-gather.13.cloned.1.call-start = ((), (), s32[]{:S(2)}) async-start(), calls=%async_computation.6 | async-start | bytes 3244032 | tf_op jit(solution)/shard_map/all_gather | solution.py:205
  12.5 418.7 %reduce-scatter.5.cloned.1.call-start = ((), (), s32[]{:S(2)}) async-start(), calls=%async_computation.7 | async-start | bytes 4325376 | tf_op jit(solution)/shard_map/reduce_scatter | solution.py:118
  172.8 52.5 %copy-start.1 = (f32[2,192,128]{2,1,0:T(8,128)}, f32[2,192,128]{2,1,0:T(8,128)S(1)}, u32[]{:S(2)}) copy-start(f32[2,192,128]{2,1,0:T(8,128)S(1)} %get-tuple-element.428) | copy-start | bytes 589828
  225.3 207.4 %reduce-scatter.3.cloned.1.call-start = ((), (), s32[]{:S(2)}) async-start(), calls=%async_computation.4 | async-start | bytes 1769472 | tf_op jit(solution)/shard_map/reduce_scatter | solution.py:112
Sparse Core Ops, SparseCore 0:
  10.6 54.2 all-gather.6
  67.4 49.5 all-gather.8
  119.5 49.5 all-gather.10
  172.1 49.5 all-gather.12
  225.5 86.9 reduce-scatter.4
  360.5 35.0 reduce-scatter.2
where the time goes:
time: 444 us; the launch traced here: 440 us
  local copies, waits for them, and re-layouts  107 us (24%)
  matrix products  107 us (24%)
  waiting for transfers between devices  98.9 us (22%)
  other arithmetic  64.3 us (14%)
  blocking collectives  45.7 us (10%)
  between operations  14.3 us (3%)
    dynamic_slice x132, local copies, waits for them, and re-layouts, over_tiles(): result, unused = lax.scan(advance, carried, (stacked, offsets))  92.4 us
    all_gather x1, waiting for transfers between devices, shards(): lax.all_gather(key_states, 'seq', axis=0, tiled=True)  49.3 us
    all_gather x1, waiting for transfers between devices, shards(): lax.all_gather(value_states, 'seq', axis=0, tiled=True)  47.4 us
    dot_general x12, matrix products, key_update(): jnp.einsum('hqk,qhd->hkd', dscores, query_split, preferred_element_type=j...  24.4 us
    dot_general x12, matrix products, query_update(): jnp.einsum('hqk,khd->hqd', dscores, key_split, preferred_element_type=jnp...  24.3 us
    add x37, other arithmetic, chain_positions(): return owner_block * shard_rows + global_rows % shard_rows  23.7 us
    select_n x37, other arithmetic, chain_positions(): block_index = global_rows // shard_rows  23.6 us
    all_gather x1, blocking collectives, shards(): lax.all_gather(log_rows, 'seq', axis=0, tiled=True)  23.5 us
  transfers between devices with their start and end apart: 6, of which 2 were waited for; matrix products, arithmetic and copies ran while one was open for 63% of the time, Pallas kernels for 0%

commit v1 on v0

v1 whole, which is shorter than its diff:
```python
import math

import jax
import jax.numpy as jnp
from jax import lax
from jax.experimental import pallas as pl
from jax.experimental.pallas import tpu as pltpu
from jax.sharding import PartitionSpec as P

F32 = jnp.float32
BF16 = jnp.bfloat16
MESH = pl.DeviceIdType.MESH
HEAD = 128
TOK = 192
CHIP = 2 * TOK
HALF = TOK // 2
N_Z = 8
SCALE = 1.0 / math.sqrt(HEAD)
SCALE2 = SCALE * math.log2(math.e)
NEG = -1e30

RIGHT, LEFT, DOWN, UP = (0, 1), (0, -1), (1, 0), (-1, 0)
EVEN, ODD = (0, TOK), (TOK, TOK)
EVEN_TOP, EVEN_LOW = (0, HALF), (HALF, HALF)
ODD_TOP, ODD_LOW = (TOK, HALF), (TOK + HALF, HALF)
WHOLE = (0, CHIP)

HOPS = [
    [((0, 0), WHOLE, d) for d in (RIGHT, LEFT, DOWN, UP)],
    [
        ((0, -1), EVEN, RIGHT),
        ((0, -1), EVEN, DOWN),
        ((0, -1), EVEN, UP),
        ((0, 1), ODD, LEFT),
        ((0, 1), EVEN, DOWN),
        ((0, 1), EVEN, UP),
        ((-1, 0), EVEN, DOWN),
        ((-1, 0), ODD, RIGHT),
        ((-1, 0), ODD, LEFT),
        ((1, 0), ODD, UP),
        ((1, 0), ODD, RIGHT),
        ((1, 0), ODD, LEFT),
    ],
    [
        ((0, 2), EVEN, DOWN),
        ((0, 2), EVEN, UP),
        ((2, 0), ODD, RIGHT),
        ((2, 0), ODD, LEFT),
        ((-1, -1), EVEN_TOP, DOWN),
        ((-1, 1), EVEN_TOP, DOWN),
        ((1, -1), EVEN_LOW, UP),
        ((1, 1), EVEN_LOW, UP),
        ((-1, -1), ODD_TOP, RIGHT),
        ((1, -1), ODD_TOP, RIGHT),
        ((-1, 1), ODD_LOW, LEFT),
        ((1, 1), ODD_LOW, LEFT),
    ],
    [
        ((-1, 2), EVEN_TOP, DOWN),
        ((1, 2), EVEN_LOW, UP),
        ((2, -1), ODD_TOP, RIGHT),
        ((2, 1), ODD_LOW, LEFT),
    ],
]
FIRST = [0, 4, 16, 28]
N_COPIES = 32
GROUPS = [
    [(0, 0), (0, -1), (0, 1), (-1, 0), (1, 0)],
    [(0, 2), (2, 0), (-1, -1), (-1, 1), (1, -1), (1, 1)],
    [(-1, 2), (1, 2), (2, -1), (2, 1), (2, 2)],
]


def dot(a, b):
    return jnp.dot(a, b, preferred_element_type=F32)


def dot_nt(a, b):
    return lax.dot_general(a, b, (((1,), (1,)), ((), ())), preferred_element_type=F32)


def wrap(value, size):
    return lax.rem(value + 2 * size, size)


def kernel(
    q_hbm, k_hbm, v_hbm, w_hbm, gy_hbm, order,
    out_ref, dq_ref, dk_ref, dv_ref, gw_ref,
    kv, qd, wv, gyc, wc, ag, gb, r1, h1, r2, gf, st, attb, dstage, swap, gswap,
    m, l, acc, dq, dk, dv,
    kv_s, kv_r, qd_s, qd_r, loc, sib_s, sib_r, wz_s, wz_r, ws_s, ws_r, st_s, st_r,
    az_s, az_r, g1_s, g1_r, g2_s, g2_r,
):
    s = lax.axis_index("seq")
    z = lax.axis_index("head")
    y = s // 8
    x = lax.rem(s // 2, 4)
    c = lax.rem(s, 2)
    chip = y * 4 + x
    twin = (s + 1 - 2 * c, z)
    o = 1 - c

    def at(step):
        return ((wrap(y + step[0], 4) * 4 + wrap(x + step[1], 4)) * 2 + c, z)

    def chip_at(step):
        return wrap(y + step[0], 4) * 4 + wrap(x + step[1], 4)

    def rows(step, part=WHOLE):
        return pl.ds(pl.multiple_of(chip_at(step) * CHIP + part[0], 32), part[1])

    def cols(index, size=HEAD):
        return pl.ds(pl.multiple_of(index * size, size), size)

    def remote(src, dst, send, recv, device):
        return pltpu.make_async_remote_copy(
            src_ref=src, dst_ref=dst, send_sem=send, recv_sem=recv, device_id=device, device_id_type=MESH
        )

    sent = []

    def send(src, dst, ssem, rsem, device):
        copy = remote(src, dst, ssem, rsem, device)
        copy.start()
        sent.append(copy)

    def arrived(dst, ssem, rsem):
        remote(dst, dst, ssem, rsem, twin).wait_recv()

    def hop_send(buf, ssem, rsem, hop, which):
        for i in which:
            step, part, way = HOPS[hop][i]
            place = buf.at[rows(step, part)]
            n = FIRST[hop] + i
            send(place, place, ssem.at[n], rsem.at[n], at(way))

    def hop_wait(buf, ssem, rsem, hop, which):
        for i in which:
            step, part, way = HOPS[hop][i]
            place = buf.at[rows((step[0] - way[0], step[1] - way[1]), part)]
            n = FIRST[hop] + i
            arrived(place, ssem.at[n], rsem.at[n])

    mine = pl.ds(pl.multiple_of(s * TOK, 32), TOK)
    half = pl.ds(pl.multiple_of(c * TOK, 32), TOK)
    other_half = pl.ds(pl.multiple_of(o * TOK, 32), TOK)
    local = [
        pltpu.make_async_copy(k_hbm.at[:, cols(c)], kv.at[mine, 0:HEAD], loc.at[0]),
        pltpu.make_async_copy(v_hbm.at[:, cols(c)], kv.at[mine, HEAD : 2 * HEAD], loc.at[1]),
        pltpu.make_async_copy(q_hbm.at[:, cols(c)], qd.at[mine, 0:HEAD], loc.at[2]),
        pltpu.make_async_copy(w_hbm, wv, loc.at[3]),
        pltpu.make_async_copy(gy_hbm, gyc.at[half], loc.at[4]),
        pltpu.make_async_copy(w_hbm.at[:, cols(z, 512)], wc.at[z], loc.at[5]),
    ]
    for copy in local:
        copy.start()
    m[...] = jnp.full_like(m, NEG)
    for ref in (l, acc, dq, dk, dv):
        ref[...] = jnp.zeros_like(ref)

    barrier = pltpu.get_barrier_semaphore()
    peers = [twin]
    for d in (1, 2, 3):
        peers += [at((0, d)), at((d, 0))]
    for d in range(1, N_Z):
        peers.append((s, wrap(z + d, N_Z)))
    for peer in peers:
        pl.semaphore_signal(barrier, inc=1, device_id=peer, device_id_type=MESH)
    pl.semaphore_wait(barrier, len(peers))

    send(k_hbm.at[:, cols(o)], kv.at[mine, 0:HEAD], sib_s.at[0], sib_r.at[0], twin)
    send(v_hbm.at[:, cols(o)], kv.at[mine, HEAD : 2 * HEAD], sib_s.at[1], sib_r.at[1], twin)
    send(q_hbm.at[:, cols(o)], qd.at[mine, 0:HEAD], sib_s.at[2], sib_r.at[2], twin)
    theirs = pl.ds(pl.multiple_of((s + 1 - 2 * c) * TOK, 32), TOK)
    local[0].wait()
    local[1].wait()
    arrived(kv.at[theirs, 0:HEAD], sib_s.at[0], sib_r.at[0])
    arrived(kv.at[theirs, HEAD : 2 * HEAD], sib_s.at[1], sib_r.at[1])
    hop_send(kv, kv_s, kv_r, 0, range(4))
    for d in range(1, N_Z):
        far = wrap(z + d, N_Z)
        send(
            w_hbm.at[cols(c), cols(far, 512)], wc.at[z, cols(c)], wz_s.at[d - 1], wz_r.at[d - 1], (s, far)
        )
    send(gy_hbm, gyc.at[half], sib_s.at[4], sib_r.at[4], twin)

    local[3].wait()
    local[4].wait()
    d_own = dot_nt(gyc[half, :], wv[...]).astype(BF16)
    dstage[0] = jnp.where(c == 0, d_own[:, 0:HEAD], d_own[:, HEAD:])
    dstage[1] = jnp.where(c == 0, d_own[:, HEAD:], d_own[:, 0:HEAD])
    qd[mine, HEAD : 2 * HEAD] = dstage[0]
    send(dstage.at[1], qd.at[mine, HEAD : 2 * HEAD], sib_s.at[3], sib_r.at[3], twin)

    def block_pos(index):
        return order[index] * TOK

    def row_pos(chips):
        lane = lax.broadcasted_iota(jnp.int32, (1, CHIP), 1)
        parts = [
            jnp.where(lane < TOK, block_pos(2 * n), block_pos(2 * n + 1) - TOK) + lane for n in chips
        ]
        return jnp.concatenate(parts, axis=1)

    def col_pos(a):
        return lax.broadcasted_iota(jnp.int32, (TOK, 1), 0) + block_pos(2 * chip + a)

    def own_rows(a):
        return pl.ds(pl.multiple_of(chip * CHIP + a * TOK, 32), TOK)

    def chip_rows(n):
        return pl.ds(pl.multiple_of(n * CHIP, 128), CHIP)

    def forward(chips):
        keys = jnp.concatenate([kv[chip_rows(n), 0:HEAD] for n in chips], axis=0)
        values = jnp.concatenate([kv[chip_rows(n), HEAD : 2 * HEAD] for n in chips], axis=0)
        key_pos = row_pos(chips)
        for a in range(2):
            rs = slice(a * TOK, (a + 1) * TOK)
            scores = dot_nt(qd[own_rows(a), 0:HEAD], keys) * SCALE2
            scores = jnp.where(key_pos <= col_pos(a), scores, NEG)
            before = m[rs, 0:1]
            now = jnp.maximum(before, jnp.max(scores, axis=1, keepdims=True))
            factor = jnp.exp2(before - now)
            weights = jnp.exp2(scores - now)
            m[rs, :] = jnp.broadcast_to(now, (TOK, HEAD))
            total = weights[:, 0:HEAD]
            for t in range(1, weights.shape[1] // HEAD):
                total = total + weights[:, t * HEAD : (t + 1) * HEAD]
            l[rs, :] = l[rs, :] * factor + total
            acc[rs, :] = acc[rs, :] * factor + dot(weights.astype(BF16), values)

    def query_grad(chips):
        keys = jnp.concatenate([kv[chip_rows(n), 0:HEAD] for n in chips], axis=0)
        values = jnp.concatenate([kv[chip_rows(n), HEAD : 2 * HEAD] for n in chips], axis=0)
        key_pos = row_pos(chips)
        for a in range(2):
            rs = slice(a * TOK, (a + 1) * TOK)
            scores = dot_nt(qd[own_rows(a), 0:HEAD], keys) * SCALE2 - m[rs, 0:1]
            probs = jnp.exp2(jnp.where(key_pos <= col_pos(a), scores, NEG))
            slopes = dot_nt(qd[own_rows(a), HEAD : 2 * HEAD], values)
            dscore = (probs * (slopes - l[rs, 0:1])).astype(BF16)
            dq[rs, :] += dot(dscore, keys)

    def key_grad(chips):
        queries = jnp.concatenate([qd[chip_rows(n), 0:HEAD] for n in chips], axis=0)
        douts = jnp.concatenate([qd[chip_rows(n), HEAD : 2 * HEAD] for n in chips], axis=0)
        query_pos = row_pos(chips)
        norm = jnp.concatenate([st[n, 0:1, :] for n in chips], axis=1)
        delta = jnp.concatenate([st[n, 1:2, :] for n in chips], axis=1)
        for a in range(2):
            rs = slice(a * TOK, (a + 1) * TOK)
            scores = dot_nt(kv[own_rows(a), 0:HEAD], queries) * SCALE2 - norm
            probs = jnp.exp2(jnp.where(col_pos(a) <= query_pos, scores, NEG))
            dv[rs, :] += dot(probs.astype(BF16), douts)
            slopes = dot_nt(kv[own_rows(a), HEAD : 2 * HEAD], douts)
            dscore = (probs * (slopes - delta)).astype(BF16)
            dk[rs, :] += dot(dscore, queries)

    hop_wait(kv, kv_s, kv_r, 0, range(4))
    hop_send(kv, kv_s, kv_r, 1, range(12))
    local[2].wait()
    arrived(qd.at[theirs, 0:HEAD], sib_s.at[2], sib_r.at[2])
    forward([chip_at(step) for step in GROUPS[0]])

    hop_wait(kv, kv_s, kv_r, 1, range(12))
    hop_send(kv, kv_s, kv_r, 2, range(12))
    arrived(qd.at[theirs, HEAD : 2 * HEAD], sib_s.at[3], sib_r.at[3])
    hop_send(qd, qd_s, qd_r, 0, range(4))
    forward([chip_at(step) for step in GROUPS[1]])

    hop_wait(kv, kv_s, kv_r, 2, range(12))
    hop_send(kv, kv_s, kv_r, 3, range(4))
    hop_wait(qd, qd_s, qd_r, 0, range(4))
    hop_send(qd, qd_s, qd_r, 1, range(12))
    hop_wait(kv, kv_s, kv_r, 3, range(4))
    forward([chip_at(step) for step in GROUPS[2]])

    for a in range(2):
        rs = slice(a * TOK, (a + 1) * TOK)
        denominator = jnp.sum(l[rs, :], axis=1, keepdims=True)
        attention = (acc[rs, :] / denominator).astype(BF16)
        attb[rs, :] = attention
        grads = qd[own_rows(a), HEAD : 2 * HEAD].astype(F32)
        delta = jnp.sum(grads * attention.astype(F32), axis=1, keepdims=True)
        m[rs, :] = jnp.broadcast_to(m[rs, 0:1] + jnp.log2(denominator), (TOK, HEAD))
        l[rs, :] = jnp.broadcast_to(delta, (TOK, HEAD))
    lane = lax.broadcasted_iota(jnp.int32, (CHIP, HEAD), 1)
    st[chip] = jnp.transpose(jnp.where(lane == 0, m[...], l[...]))[0:8, :]

    send(st.at[chip], st.at[chip], st_s.at[0], st_r.at[0], at(RIGHT))
    send(st.at[chip], st.at[chip], st_s.at[1], st_r.at[1], at(LEFT))
    own_att = pltpu.make_async_copy(attb.at[half], ag.at[z, :, cols(c)], loc.at[6])
    own_att.start()
    send(attb.at[other_half], ag.at[z, :, cols(c)], sib_s.at[5], sib_r.at[5], twin)

    arrived(gyc.at[other_half], sib_s.at[4], sib_r.at[4])
    att_t = jnp.transpose(attb[...].astype(F32)).astype(BF16)

    @pl.loop(0, 16)
    def _(n):
        part = dot(att_t, gyc[:, pl.ds(pl.multiple_of(n * 256, 256), 256)])
        gb[n // 4, lax.rem(n, 4)] = part.astype(BF16)

    own_att.wait()
    arrived(ag.at[z, :, cols(o)], sib_s.at[5], sib_r.at[5])

    def z_at(step):
        return wrap(z + step, N_Z)

    def z_hop(n, block, way, part=None):
        place = ag.at[z_at(block)] if part is None else ag.at[z_at(block), part]
        send(place, place, az_s.at[n], az_r.at[n], (s, z_at(way)))

    def z_wait(n, block, part=None):
        place = ag.at[z_at(block)] if part is None else ag.at[z_at(block), part]
        arrived(place, az_s.at[n], az_r.at[n])

    top, low = slice(0, HALF), slice(HALF, TOK)
    z_hop(0, 0, 1)
    z_hop(1, 0, -1)

    upper, lower = slice(0, 64), slice(64, 128)
    for d in (1, 2, 3):
        send(gb.at[:, wrap(x + d, 4), upper], r1.at[0, d - 1], g1_s.at[0, d - 1], g1_r.at[0, d - 1], at((0, d)))
        send(gb.at[wrap(y + d, 4), :, lower], r1.at[1, d - 1], g1_s.at[1, d - 1], g1_r.at[1, d - 1], at((d, 0)))

    def st_row(step):
        return st.at[pl.ds(wrap(y + step, 4) * 4, 4)]

    def st_at(step):
        return st.at[chip_at(step)]

    arrived(st_at((0, -1)), st_s.at[0], st_r.at[0])
    send(st_at((0, -1)), st_at((0, -1)), st_s.at[2], st_r.at[2], at(RIGHT))
    query_grad(list(range(0, 4)))
    arrived(st_at((0, 1)), st_s.at[1], st_r.at[1])
    arrived(st_at((0, 2)), st_s.at[2], st_r.at[2])
    send(st_row(0), st_row(0), st_s.at[3], st_r.at[3], at(DOWN))
    send(st_row(0), st_row(0), st_s.at[4], st_r.at[4], at(UP))
    z_wait(0, -1)
    z_hop(2, -1, 1)
    z_wait(1, 1)
    z_hop(3, 1, -1)
    query_grad(list(range(4, 8)))
    for d in range(1, N_Z):
        place = wc.at[z_at(-d), cols(c)]
        arrived(place, wz_s.at[d - 1], wz_r.at[d - 1])
        send(place, place, ws_s.at[d - 1], ws_r.at[d - 1], twin)
    hop_wait(qd, qd_s, qd_r, 1, range(12))
    hop_send(qd, qd_s, qd_r, 2, range(12))
    arrived(st_row(-1), st_s.at[3], st_r.at[3])
    send(st_row(-1), st_row(-1), st_s.at[5], st_r.at[5], at(DOWN))
    z_wait(2, -2)
    z_hop(4, -2, 1)
    z_wait(3, 2)
    z_hop(5, 2, -1)
    query_grad(list(range(8, 12)))
    arrived(st_row(1), st_s.at[4], st_r.at[4])
    arrived(st_row(2), st_s.at[5], st_r.at[5])
    query_grad(list(range(12, 16)))

    for way in range(2):
        for d in (1, 2, 3):
            arrived(r1.at[way, d - 1], g1_s.at[way, d - 1], g1_r.at[way, d - 1])
    for n in range(4):
        total = gb[n, x, upper].astype(F32)
        for d in range(3):
            total = total + r1[0, d, n].astype(F32)
        h1[0, n] = total.astype(BF16)
        total = gb[y, n, lower].astype(F32)
        for d in range(3):
            total = total + r1[1, d, n].astype(F32)
        h1[1, n] = total.astype(BF16)
    for d in (1, 2, 3):
        send(h1.at[0, wrap(y + d, 4)], r2.at[0, d - 1], g2_s.at[0, d - 1], g2_r.at[0, d - 1], at((d, 0)))
        send(h1.at[1, wrap(x + d, 4)], r2.at[1, d - 1], g2_s.at[1, d - 1], g2_r.at[1, d - 1], at((0, d)))

    key_grad([chip_at(step) for step in GROUPS[0]])
    z_wait(4, -3)
    z_hop(6, -3, 1, top)
    z_wait(5, 3)
    z_hop(7, 3, -1, low)
    key_grad([chip_at(step) for step in GROUPS[1]])
    hop_wait(qd, qd_s, qd_r, 2, range(12))
    hop_send(qd, qd_s, qd_r, 3, range(4))

    for way in range(2):
        for d in (1, 2, 3):
            arrived(r2.at[way, d - 1], g2_s.at[way, d - 1], g2_r.at[way, d - 1])
    for way, own in ((0, y), (1, x)):
        total = h1[way, own].astype(F32)
        for d in range(3):
            total = total + r2[way, d].astype(F32)
        total = total.astype(BF16)
        rs = slice(way * 64, way * 64 + 64)
        gf[0, rs, :] = jnp.where(c == 0, total[:, 0:HEAD], total[:, HEAD:])
        gf[1, rs, :] = jnp.where(c == 0, total[:, HEAD:], total[:, 0:HEAD])
    send(gf.at[1], gswap, sib_s.at[6], sib_r.at[6], twin)

    for d in range(1, N_Z):
        arrived(wc.at[z_at(-d), cols(o)], ws_s.at[d - 1], ws_r.at[d - 1])
    z_wait(6, -4, top)
    z_wait(7, 4, low)
    local[5].wait()
    total = dot(ag[0], wc[0])
    for n in range(1, N_Z):
        total = total + dot(ag[n], wc[n])
    out_ref[...] = total.astype(BF16)

    hop_wait(qd, qd_s, qd_r, 3, range(4))
    key_grad([chip_at(step) for step in GROUPS[2]])

    for n, (ref, factor) in enumerate(((dq, SCALE), (dk, SCALE), (dv, 1.0))):
        swap[0, n] = (ref[...] * factor).astype(BF16)
        send(swap.at[0, n, other_half], swap.at[1, n, 0:TOK], sib_s.at[7 + n], sib_r.at[7 + n], twin)
    arrived(gswap, sib_s.at[6], sib_r.at[6])
    gw_ref[0:HEAD, :] = jnp.where(c == 0, gf[0], gswap[...])
    gw_ref[HEAD : 2 * HEAD, :] = jnp.where(c == 0, gswap[...], gf[0])
    for n, ref in enumerate((dq_ref, dk_ref, dv_ref)):
        arrived(swap.at[1, n, 0:TOK], sib_s.at[7 + n], sib_r.at[7 + n])
        own = swap[0, n, half, :]
        other = swap[1, n, 0:TOK, :]
        ref[:, 0:HEAD] = jnp.where(c == 0, own, other)
        ref[:, HEAD : 2 * HEAD] = jnp.where(c == 0, other, own)
    for copy in sent:
        copy.wait_send()


def shards(queries, key_states, value_states, w_out, grad_y, chain_order):
    anywhere = pl.BlockSpec(memory_space=pl.ANY)
    vmem = pl.BlockSpec(memory_space=pltpu.VMEM)
    dma = pltpu.SemaphoreType.DMA
    tokens = 32 * TOK
    tile = jax.ShapeDtypeStruct((TOK, 2 * HEAD), BF16)
    scratch = [
        pltpu.VMEM((tokens, 2 * HEAD), BF16),
        pltpu.VMEM((tokens, 2 * HEAD), BF16),
        pltpu.VMEM((2 * HEAD, 4096), BF16),
        pltpu.VMEM((CHIP, 4096), BF16),
        pltpu.VMEM((N_Z, 2 * HEAD, 512), BF16),
        pltpu.VMEM((N_Z, TOK, 2 * HEAD), BF16),
        pltpu.VMEM((4, 4, HEAD, 256), BF16),
        pltpu.VMEM((2, 3, 4, 64, 256), BF16),
        pltpu.VMEM((2, 4, 64, 256), BF16),
        pltpu.VMEM((2, 3, 64, 256), BF16),
        pltpu.VMEM((2, HEAD, HEAD), BF16),
        pltpu.VMEM((16, 8, CHIP), F32),
        pltpu.VMEM((CHIP, HEAD), BF16),
        pltpu.VMEM((2, TOK, HEAD), BF16),
        pltpu.VMEM((2, 3, CHIP, HEAD), BF16),
        pltpu.VMEM((HEAD, HEAD), BF16),
    ]
    scratch += [pltpu.VMEM((CHIP, HEAD), F32)] * 6
    scratch += [dma((N_COPIES,))] * 4
    scratch += [dma((7,)), dma((10,)), dma((10,))]
    scratch += [dma((7,))] * 4
    scratch += [dma((6,))] * 2
    scratch += [dma((8,))] * 2
    scratch += [dma((2, 3))] * 4
    return pl.pallas_call(
        kernel,
        out_shape=(
            jax.ShapeDtypeStruct((TOK, 512), BF16),
            tile,
            tile,
            tile,
            jax.ShapeDtypeStruct((2 * HEAD, HEAD), BF16),
        ),
        in_specs=[anywhere] * 5 + [pl.BlockSpec(memory_space=pltpu.SMEM)],
        out_specs=(vmem,) * 5,
        scratch_shapes=scratch,
        compiler_params=pltpu.CompilerParams(
            collective_id=0, has_side_effects=True, vmem_limit_bytes=56 * 1024 * 1024
        ),
        name="attention_layer",
    )(queries, key_states, value_states, w_out, grad_y, chain_order)


def solution(mesh):
    return jax.shard_map(
        shards,
        mesh=mesh,
        in_specs=(
            P("seq", "head"),
            P("seq", "head"),
            P("seq", "head"),
            P("head", None),
            P("seq", None),
            P(),
        ),
        out_specs=(
            P("seq", "head"),
            P("seq", "head"),
            P("seq", "head"),
            P("seq", "head"),
            P("head", "seq"),
        ),
        check_vma=False,
    )
```

time: 444 us -> 85 us (0.19)
  matrix products: 107 us -> 0 us
  local copies, waits for them, and re-layouts: 107 us -> 7.7 us
  waiting for transfers between devices: 98.9 us -> 0 us
  Pallas kernels: 0 us -> 76.4 us
  other arithmetic: 64.3 us -> 0 us
  blocking collectives: 45.7 us -> 0 us
  between operations: 14.3 us -> 0.64 us
    dot_general x87 -> x0, matrix products: 107 us -> none  [the longest x12 24.4 us: key_update(): jnp.einsum('hqk,qhd->hkd', dscores, query_split, preferred_element_type=j...]
    all_gather x4 -> x0, waiting for transfers between devices: 96.8 us -> none  [the longest x1 49.3 us: shards(): lax.all_gather(key_states, 'seq', axis=0, tiled=True)]
    dynamic_slice x132 -> x0, local copies, waits for them, and re-layouts: 92.4 us -> none  [over_tiles(): result, unused = lax.scan(advance, carried, (stacked, offsets))]
    pallas_call x0 -> x1, Pallas kernels: none -> 76.4 us  [shards(): pl.pallas_call(kernel, out_shape=(jax.ShapeDtypeStruct((TOK, 512), BF16),...]
    all_gather x2 -> x0, blocking collectives: 45.7 us -> none  [the longest x1 23.5 us: shards(): lax.all_gather(log_rows, 'seq', axis=0, tiled=True)]
    add x50 -> x0, other arithmetic: 24 us -> none  [the longest x37 23.7 us: chain_positions(): return owner_block * shard_rows + global_rows % shard_rows]
    select_n x37 -> x0, other arithmetic: 23.6 us -> none  [chain_positions(): block_index = global_rows // shard_rows]
    reduce_sum x50 -> x0, other arithmetic: 8.03 us -> none  [the longest x12 3.57 us: forward_update(): denominator = denominator * factor + jnp.sum(weights, axis=2)]
  transfers between devices with their start and end apart: 6 -> 0, of which waited for: 2 -> 0; matrix products, arithmetic and copies ran while one was open for 63% -> 0% of each run, Pallas kernels for 0% -> 0%
where the time goes in v1:
time: 85 us; the launch traced here: 84.8 us
  Pallas kernels  76.4 us (90%)
  local copies, waits for them, and re-layouts  7.7 us (9%)
    pallas_call x1, Pallas kernels, shards(): pl.pallas_call(kernel, out_shape=(jax.ShapeDtypeStruct((TOK, 512), BF16),...  76.4 us
    unnamed x5, local copies, waits for them, and re-layouts  7.7 us

profile of v1, /device:TPU:1, one launch (start us, length us, event | category | flops | bytes accessed | tf_op | source)
XLA Modules:
  0.0 84.8 jit_solution(1432684610358043237)
XLA Ops:
  0.6 76.4 %attention_layer.1 = (bf16[192,512]{1,0:T(8,128)(2,1)}, bf16[192,256]{1,0:T(8,128)(2,1)}, bf16[192,256]{1,0:T(8,128)(2,1)}, bf16[192,256]{1,0:T(8,128)(2,1)}, bf16[256,128]{1,0:T(8,128)(2,1)}) custom-call(bf16[192,256]{1,0:T(8,128)(2,1)} %q_hbm.1, bf16[192,256]{1,0:T(8,128)(2,1)} %k_hbm.1, bf16[192,256]{1,0:T(8,128)(2,1)} %v_hbm.1, bf16[256,4096]{1,0:T(8,128)(2,1)} %w_hbm.1, ...), custom_call_target="tpu_custom_call" | custom-call | tf_op jit(solution)/shard_map/attention_layer/pallas_call | solution.py:461
  77.0 1.6 %copy.16 = bf16[192,512]{1,0:T(8,128)(2,1)} copy(bf16[192,512]{1,0:T(8,128)(2,1)} %get-tuple-element.10) | data formatting | bytes 393216
  78.7 1.5 %copy.17 = bf16[192,256]{1,0:T(8,128)(2,1)} copy(bf16[192,256]{1,0:T(8,128)(2,1)} %get-tuple-element.11) | data formatting | bytes 196608
  80.2 1.5 %copy.18 = bf16[192,256]{1,0:T(8,128)(2,1)} copy(bf16[192,256]{1,0:T(8,128)(2,1)} %get-tuple-element.12) | data formatting | bytes 196608
  81.7 1.5 %copy.19 = bf16[192,256]{1,0:T(8,128)(2,1)} copy(bf16[192,256]{1,0:T(8,128)(2,1)} %get-tuple-element.13) | data formatting | bytes 196608
  83.3 1.5 %copy.20 = bf16[256,128]{1,0:T(8,128)(2,1)} copy(bf16[256,128]{1,0:T(8,128)(2,1)} %get-tuple-element.14) | data formatting | bytes 131072

commit v2 on v1

--- a/solution.py
+++ b/solution.py
@@ -25,45 +25,50 @@
 ODD_TOP, ODD_LOW = (TOK, HALF), (TOK + HALF, HALF)
 WHOLE = (0, CHIP)
 
-HOPS = [
-    [((0, 0), WHOLE, d) for d in (RIGHT, LEFT, DOWN, UP)],
+FLOWS = [
     [
-        ((0, -1), EVEN, RIGHT),
-        ((0, -1), EVEN, DOWN),
-        ((0, -1), EVEN, UP),
-        ((0, 1), ODD, LEFT),
-        ((0, 1), EVEN, DOWN),
-        ((0, 1), EVEN, UP),
-        ((-1, 0), EVEN, DOWN),
-        ((-1, 0), ODD, RIGHT),
-        ((-1, 0), ODD, LEFT),
-        ((1, 0), ODD, UP),
-        ((1, 0), ODD, RIGHT),
-        ((1, 0), ODD, LEFT),
+        [((0, 0), EVEN, d) for d in (RIGHT, LEFT, DOWN, UP)],
+        [
+            ((0, -1), EVEN, DOWN),
+            ((0, -1), EVEN, UP),
+            ((0, -1), EVEN, RIGHT),
+            ((0, 1), EVEN, DOWN),
+            ((0, 1), EVEN, UP),
+            ((-1, 0), EVEN, DOWN),
+        ],
+        [
+            ((0, 2), EVEN, DOWN),
+            ((0, 2), EVEN, UP),
+            ((-1, -1), EVEN_TOP, DOWN),
+            ((-1, 1), EVEN_TOP, DOWN),
+            ((1, -1), EVEN_LOW, UP),
+            ((1, 1), EVEN_LOW, UP),
+        ],
+        [((-1, 2), EVEN_TOP, DOWN), ((1, 2), EVEN_LOW, UP)],
     ],
     [
-        ((0, 2), EVEN, DOWN),
-        ((0, 2), EVEN, UP),
-        ((2, 0), ODD, RIGHT),
-        ((2, 0), ODD, LEFT),
-        ((-1, -1), EVEN_TOP, DOWN),
-        ((-1, 1), EVEN_TOP, DOWN),
-        ((1, -1), EVEN_LOW, UP),
-        ((1, 1), EVEN_LOW, UP),
-        ((-1, -1), ODD_TOP, RIGHT),
-        ((1, -1), ODD_TOP, RIGHT),
-        ((-1, 1), ODD_LOW, LEFT),
-        ((1, 1), ODD_LOW, LEFT),
-    ],
-    [
-        ((-1, 2), EVEN_TOP, DOWN),
-        ((1, 2), EVEN_LOW, UP),
-        ((2, -1), ODD_TOP, RIGHT),
-        ((2, 1), ODD_LOW, LEFT),
+        [((0, 0), ODD, d) for d in (RIGHT, LEFT, DOWN, UP)],
+        [
+            ((1, 0), ODD, RIGHT),
+            ((1, 0), ODD, LEFT),
+            ((1, 0), ODD, UP),
+            ((-1, 0), ODD, RIGHT),
+            ((-1, 0), ODD, LEFT),
+            ((0, 1), ODD, LEFT),
+        ],
+        [
+            ((2, 0), ODD, RIGHT),
+            ((2, 0), ODD, LEFT),
+            ((-1, -1), ODD_TOP, RIGHT),
+            ((1, -1), ODD_TOP, RIGHT),
+            ((-1, 1), ODD_LOW, LEFT),
+            ((1, 1), ODD_LOW, LEFT),
+        ],
+        [((2, -1), ODD_TOP, RIGHT), ((2, 1), ODD_LOW, LEFT)],
     ],
 ]
-FIRST = [0, 4, 16, 28]
-N_COPIES = 32
+FIRST = [0, 4, 10, 16]
+N_COPIES = 18
 GROUPS = [
     [(0, 0), (0, -1), (0, 1), (-1, 0), (1, 0)],
     [(0, 2), (2, 0), (-1, -1), (-1, 1), (1, -1), (1, 1)],
@@ -86,10 +91,10 @@
 def kernel(
     q_hbm, k_hbm, v_hbm, w_hbm, gy_hbm, order,
     out_ref, dq_ref, dk_ref, dv_ref, gw_ref,
-    kv, qd, wv, gyc, wc, ag, gb, r1, h1, r2, gf, st, attb, dstage, swap, gswap,
+    kv, qd, wv, gyc, wc, ag, gb, r1, h1, r2, gf, st, attb, kvs, qds, swap, gswap,
     m, l, acc, dq, dk, dv,
-    kv_s, kv_r, qd_s, qd_r, loc, sib_s, sib_r, wz_s, wz_r, ws_s, ws_r, st_s, st_r,
-    az_s, az_r, g1_s, g1_r, g2_s, g2_r,
+    kv_s, kv_r, qd_s, qd_r, own_s, own_r, loc, sib_s, sib_r, wz_s, wz_r, ws_s, ws_r, st_s, st_r,
+    az_s, az_r, a0_s, a0_r, g1_s, g1_r, g2_s, g2_r,
 ):
     s = lax.axis_index("seq")
     z = lax.axis_index("head")
@@ -127,30 +132,38 @@
     def arrived(dst, ssem, rsem):
         remote(dst, dst, ssem, rsem, twin).wait_recv()
 
-    def hop_send(buf, ssem, rsem, hop, which):
-        for i in which:
-            step, part, way = HOPS[hop][i]
-            place = buf.at[rows(step, part)]
+    def same(a, b):
+        return (a[0] - b[0]) % 4 == 0 and (a[1] - b[1]) % 4 == 0
+
+    def hop_send(buf, ssem, rsem, flow, hop, step=None):
+        for i, (source, part, way) in enumerate(FLOWS[flow][hop]):
+            if step is None or same(step, source):
+                place = buf.at[rows(source, part)]
+                n = FIRST[hop] + i
+                send(place, place, ssem.at[flow, n], rsem.at[flow, n], at(way))
+
+    def relay(buf, ssem, rsem, flow, hop):
+        for i, (source, part, way) in enumerate(FLOWS[flow][hop]):
+            step = (source[0] - way[0], source[1] - way[1])
             n = FIRST[hop] + i
-            send(place, place, ssem.at[n], rsem.at[n], at(way))
-
-    def hop_wait(buf, ssem, rsem, hop, which):
-        for i in which:
-            step, part, way = HOPS[hop][i]
-            place = buf.at[rows((step[0] - way[0], step[1] - way[1]), part)]
-            n = FIRST[hop] + i
-            arrived(place, ssem.at[n], rsem.at[n])
+            arrived(buf.at[rows(step, part)], ssem.at[flow, n], rsem.at[flow, n])
+            if hop < 3:
+                hop_send(buf, ssem, rsem, flow, hop + 1, step)
 
     mine = pl.ds(pl.multiple_of(s * TOK, 32), TOK)
     half = pl.ds(pl.multiple_of(c * TOK, 32), TOK)
     other_half = pl.ds(pl.multiple_of(o * TOK, 32), TOK)
-    local = [
-        pltpu.make_async_copy(k_hbm.at[:, cols(c)], kv.at[mine, 0:HEAD], loc.at[0]),
-        pltpu.make_async_copy(v_hbm.at[:, cols(c)], kv.at[mine, HEAD : 2 * HEAD], loc.at[1]),
-        pltpu.make_async_copy(q_hbm.at[:, cols(c)], qd.at[mine, 0:HEAD], loc.at[2]),
-        pltpu.make_async_copy(w_hbm, wv, loc.at[3]),
-        pltpu.make_async_copy(gy_hbm, gyc.at[half], loc.at[4]),
-        pltpu.make_async_copy(w_hbm.at[:, cols(z, 512)], wc.at[z], loc.at[5]),
+    local = []
+    for h in range(2):
+        local += [
+            pltpu.make_async_copy(k_hbm.at[:, cols(h)], kvs.at[h, :, 0:HEAD], loc.at[3 * h]),
+            pltpu.make_async_copy(v_hbm.at[:, cols(h)], kvs.at[h, :, HEAD : 2 * HEAD], loc.at[3 * h + 1]),
+            pltpu.make_async_copy(q_hbm.at[:, cols(h)], qds.at[h, :, 0:HEAD], loc.at[3 * h + 2]),
+        ]
+    local += [
+        pltpu.make_async_copy(w_hbm, wv, loc.at[6]),
+        pltpu.make_async_copy(gy_hbm, gyc.at[half], loc.at[7]),
+        pltpu.make_async_copy(w_hbm.at[:, cols(z, 512)], wc.at[z], loc.at[8]),
     ]
     for copy in local:
         copy.start()
@@ -159,7 +172,9 @@
         ref[...] = jnp.zeros_like(ref)
 
     barrier = pltpu.get_barrier_semaphore()
-    peers = [twin]
+    peers = [twin, (twin[0], wrap(z + 1, N_Z)), (twin[0], wrap(z - 1, N_Z))]
+    for way in (RIGHT, LEFT, DOWN, UP):
+        peers.append((chip_at(way) * 2 + o, z))
     for d in (1, 2, 3):
         peers += [at((0, d)), at((d, 0))]
     for d in range(1, N_Z):
@@ -168,15 +183,19 @@
         pl.semaphore_signal(barrier, inc=1, device_id=peer, device_id_type=MESH)
     pl.semaphore_wait(barrier, len(peers))
 
-    send(k_hbm.at[:, cols(o)], kv.at[mine, 0:HEAD], sib_s.at[0], sib_r.at[0], twin)
-    send(v_hbm.at[:, cols(o)], kv.at[mine, HEAD : 2 * HEAD], sib_s.at[1], sib_r.at[1], twin)
-    send(q_hbm.at[:, cols(o)], qd.at[mine, 0:HEAD], sib_s.at[2], sib_r.at[2], twin)
+    def first_send(buf, stage, which, ssem, rsem):
+        for i, way in enumerate((RIGHT, LEFT, DOWN, UP)):
+            for h in range(2):
+                send(stage.at[h], buf.at[mine], ssem.at[h, i], rsem.at[c, i], (chip_at(way) * 2 + h, z))
+        send(stage.at[o], buf.at[mine], own_s.at[which], own_r.at[which], twin)
+        own = pltpu.make_async_copy(stage.at[c], buf.at[mine], loc.at[9 + which])
+        own.start()
+        return own
+
     theirs = pl.ds(pl.multiple_of((s + 1 - 2 * c) * TOK, 32), TOK)
-    local[0].wait()
-    local[1].wait()
-    arrived(kv.at[theirs, 0:HEAD], sib_s.at[0], sib_r.at[0])
-    arrived(kv.at[theirs, HEAD : 2 * HEAD], sib_s.at[1], sib_r.at[1])
-    hop_send(kv, kv_s, kv_r, 0, range(4))
+    for n in (0, 1, 3, 4):
+        local[n].wait()
+    own_kv = first_send(kv, kvs, 0, kv_s, kv_r)
     for d in range(1, N_Z):
         far = wrap(z + d, N_Z)
         send(
@@ -184,13 +203,13 @@
         )
     send(gy_hbm, gyc.at[half], sib_s.at[4], sib_r.at[4], twin)
 
-    local[3].wait()
-    local[4].wait()
+    local[6].wait()
+    local[7].wait()
     d_own = dot_nt(gyc[half, :], wv[...]).astype(BF16)
-    dstage[0] = jnp.where(c == 0, d_own[:, 0:HEAD], d_own[:, HEAD:])
-    dstage[1] = jnp.where(c == 0, d_own[:, HEAD:], d_own[:, 0:HEAD])
-    qd[mine, HEAD : 2 * HEAD] = dstage[0]
-    send(dstage.at[1], qd.at[mine, HEAD : 2 * HEAD], sib_s.at[3], sib_r.at[3], twin)
+    qds[0, :, HEAD : 2 * HEAD] = d_own[:, 0:HEAD]
+    qds[1, :, HEAD : 2 * HEAD] = d_own[:, HEAD:]
+    local[2].wait()
+    local[5].wait()
 
     def block_pos(index):
         return order[index] * TOK
@@ -257,24 +276,27 @@
             dscore = (probs * (slopes - delta)).astype(BF16)
             dk[rs, :] += dot(dscore, queries)
 
-    hop_wait(kv, kv_s, kv_r, 0, range(4))
-    hop_send(kv, kv_s, kv_r, 1, range(12))
-    local[2].wait()
-    arrived(qd.at[theirs, 0:HEAD], sib_s.at[2], sib_r.at[2])
+    relay(kv, kv_s, kv_r, 0, 0)
+    relay(kv, kv_s, kv_r, 1, 0)
+    own_kv.wait()
+    arrived(kv.at[theirs], own_s.at[0], own_r.at[0])
+    own_qd = first_send(qd, qds, 1, qd_s, qd_r)
+    own_qd.wait()
+    arrived(qd.at[theirs], own_s.at[1], own_r.at[1])
     forward([chip_at(step) for step in GROUPS[0]])
 
-    hop_wait(kv, kv_s, kv_r, 1, range(12))
-    hop_send(kv, kv_s, kv_r, 2, range(12))
-    arrived(qd.at[theirs, HEAD : 2 * HEAD], sib_s.at[3], sib_r.at[3])
-    hop_send(qd, qd_s, qd_r, 0, range(4))
+    relay(kv, kv_s, kv_r, 0, 1)
+    relay(kv, kv_s, kv_r, 1, 1)
     forward([chip_at(step) for step in GROUPS[1]])
 
-    hop_wait(kv, kv_s, kv_r, 2, range(12))
-    hop_send(kv, kv_s, kv_r, 3, range(4))
-    hop_wait(qd, qd_s, qd_r, 0, range(4))
-    hop_send(qd, qd_s, qd_r, 1, range(12))
-    hop_wait(kv, kv_s, kv_r, 3, range(4))
-    forward([chip_at(step) for step in GROUPS[2]])
+    relay(kv, kv_s, kv_r, 0, 2)
+    relay(kv, kv_s, kv_r, 1, 2)
+    relay(qd, qd_s, qd_r, 0, 0)
+    relay(qd, qd_s, qd_r, 1, 0)
+    forward([chip_at(step) for step in GROUPS[2][:4]])
+    relay(kv, kv_s, kv_r, 0, 3)
+    relay(kv, kv_s, kv_r, 1, 3)
+    forward([chip_at(step) for step in GROUPS[2][4:]])
 
     for a in range(2):
         rs = slice(a * TOK, (a + 1) * TOK)
@@ -288,10 +310,20 @@
     lane = lax.broadcasted_iota(jnp.int32, (CHIP, HEAD), 1)
     st[chip] = jnp.transpose(jnp.where(lane == 0, m[...], l[...]))[0:8, :]
 
-    send(st.at[chip], st.at[chip], st_s.at[0], st_r.at[0], at(RIGHT))
-    send(st.at[chip], st.at[chip], st_s.at[1], st_r.at[1], at(LEFT))
-    own_att = pltpu.make_async_copy(attb.at[half], ag.at[z, :, cols(c)], loc.at[6])
+    for d in (1, 2, 3):
+        send(st.at[chip], st.at[chip], st_s.at[0, d - 1], st_r.at[0, d - 1], at((0, d)))
+    own_att = pltpu.make_async_copy(attb.at[half], ag.at[z, :, cols(c)], loc.at[11])
     own_att.start()
+    for part in range(2):
+        for n, step in enumerate((1, -1)):
+            for h in range(2):
+                send(
+                    attb.at[h * TOK + part * HALF : h * TOK + (part + 1) * HALF],
+                    ag.at[z, part * HALF : (part + 1) * HALF, cols(c)],
+                    a0_s.at[2 * n + part, h],
+                    a0_r.at[2 * n + part, c],
+                    (chip * 2 + h, wrap(z + step, N_Z)),
+                )
     send(attb.at[other_half], ag.at[z, :, cols(c)], sib_s.at[5], sib_r.at[5], twin)
 
     arrived(gyc.at[other_half], sib_s.at[4], sib_r.at[4])
@@ -302,23 +334,35 @@
         part = dot(att_t, gyc[:, pl.ds(pl.multiple_of(n * 256, 256), 256)])
         gb[n // 4, lax.rem(n, 4)] = part.astype(BF16)
 
-    own_att.wait()
-    arrived(ag.at[z, :, cols(o)], sib_s.at[5], sib_r.at[5])
 
     def z_at(step):
         return wrap(z + step, N_Z)
 
-    def z_hop(n, block, way, part=None):
-        place = ag.at[z_at(block)] if part is None else ag.at[z_at(block), part]
+    def z_place(block, part):
+        return ag.at[z_at(block), part * HALF : (part + 1) * HALF]
+
+    def z_send(hop, way, part):
+        place = z_place(-way * hop, part)
+        n = way_index(way), 2 * hop + part
         send(place, place, az_s.at[n], az_r.at[n], (s, z_at(way)))
 
-    def z_wait(n, block, part=None):
-        place = ag.at[z_at(block)] if part is None else ag.at[z_at(block), part]
-        arrived(place, az_s.at[n], az_r.at[n])
-
-    top, low = slice(0, HALF), slice(HALF, TOK)
-    z_hop(0, 0, 1)
-    z_hop(1, 0, -1)
+    def way_index(way):
+        return 0 if way > 0 else 1
+
+    def z_relay(hop):
+        for part in (0, 1):
+            for way in (1, -1):
+                if hop == 3 and part != way_index(way):
+                    continue
+                n = way_index(way), 2 * hop + part
+                if hop == 0:
+                    for h in range(2):
+                        place = ag.at[z_at(-way), part * HALF : (part + 1) * HALF, cols(h)]
+                        arrived(place, a0_s.at[2 * n[0] + part, h], a0_r.at[2 * n[0] + part, h])
+                else:
+                    arrived(z_place(-way * (hop + 1), part), az_s.at[n], az_r.at[n])
+                if hop < 2 or (hop == 2 and part == way_index(way)):
+                    z_send(hop + 1, way, part)
 
     upper, lower = slice(0, 64), slice(64, 128)
     for d in (1, 2, 3):
@@ -328,37 +372,32 @@
     def st_row(step):
         return st.at[pl.ds(wrap(y + step, 4) * 4, 4)]
 
-    def st_at(step):
-        return st.at[chip_at(step)]
-
-    arrived(st_at((0, -1)), st_s.at[0], st_r.at[0])
-    send(st_at((0, -1)), st_at((0, -1)), st_s.at[2], st_r.at[2], at(RIGHT))
+    def swap_send(n, ref, factor):
+        swap[0, n] = (ref[...] * factor).astype(BF16)
+        send(swap.at[0, n, other_half], swap.at[1, n, 0:TOK], sib_s.at[7 + n], sib_r.at[7 + n], twin)
+
+    relay(qd, qd_s, qd_r, 0, 1)
+    relay(qd, qd_s, qd_r, 1, 1)
+    z_relay(0)
+    for d in (1, 2, 3):
+        arrived(st.at[chip_at((0, -d))], st_s.at[0, d - 1], st_r.at[0, d - 1])
+    for d in (1, 2, 3):
+        send(st_row(0), st_row(0), st_s.at[1, d - 1], st_r.at[1, d - 1], at((d, 0)))
     query_grad(list(range(0, 4)))
-    arrived(st_at((0, 1)), st_s.at[1], st_r.at[1])
-    arrived(st_at((0, 2)), st_s.at[2], st_r.at[2])
-    send(st_row(0), st_row(0), st_s.at[3], st_r.at[3], at(DOWN))
-    send(st_row(0), st_row(0), st_s.at[4], st_r.at[4], at(UP))
-    z_wait(0, -1)
-    z_hop(2, -1, 1)
-    z_wait(1, 1)
-    z_hop(3, 1, -1)
     query_grad(list(range(4, 8)))
+    z_relay(1)
     for d in range(1, N_Z):
         place = wc.at[z_at(-d), cols(c)]
         arrived(place, wz_s.at[d - 1], wz_r.at[d - 1])
         send(place, place, ws_s.at[d - 1], ws_r.at[d - 1], twin)
-    hop_wait(qd, qd_s, qd_r, 1, range(12))
-    hop_send(qd, qd_s, qd_r, 2, range(12))
-    arrived(st_row(-1), st_s.at[3], st_r.at[3])
-    send(st_row(-1), st_row(-1), st_s.at[5], st_r.at[5], at(DOWN))
-    z_wait(2, -2)
-    z_hop(4, -2, 1)
-    z_wait(3, 2)
-    z_hop(5, 2, -1)
     query_grad(list(range(8, 12)))
-    arrived(st_row(1), st_s.at[4], st_r.at[4])
-    arrived(st_row(2), st_s.at[5], st_r.at[5])
+    relay(qd, qd_s, qd_r, 0, 2)
+    relay(qd, qd_s, qd_r, 1, 2)
+    z_relay(2)
     query_grad(list(range(12, 16)))
+    for d in (1, 2, 3):
+        arrived(st_row(-d), st_s.at[1, d - 1], st_r.at[1, d - 1])
+    swap_send(0, dq, SCALE)
 
     for way in range(2):
         for d in (1, 2, 3):
@@ -377,13 +416,7 @@
         send(h1.at[1, wrap(x + d, 4)], r2.at[1, d - 1], g2_s.at[1, d - 1], g2_r.at[1, d - 1], at((0, d)))
 
     key_grad([chip_at(step) for step in GROUPS[0]])
-    z_wait(4, -3)
-    z_hop(6, -3, 1, top)
-    z_wait(5, 3)
-    z_hop(7, 3, -1, low)
     key_grad([chip_at(step) for step in GROUPS[1]])
-    hop_wait(qd, qd_s, qd_r, 2, range(12))
-    hop_send(qd, qd_s, qd_r, 3, range(4))
 
     for way in range(2):
         for d in (1, 2, 3):
@@ -400,20 +433,21 @@
 
     for d in range(1, N_Z):
         arrived(wc.at[z_at(-d), cols(o)], ws_s.at[d - 1], ws_r.at[d - 1])
-    z_wait(6, -4, top)
-    z_wait(7, 4, low)
-    local[5].wait()
+    z_relay(3)
+    local[8].wait()
+    own_att.wait()
+    arrived(ag.at[z, :, cols(o)], sib_s.at[5], sib_r.at[5])
     total = dot(ag[0], wc[0])
     for n in range(1, N_Z):
         total = total + dot(ag[n], wc[n])
     out_ref[...] = total.astype(BF16)
 
-    hop_wait(qd, qd_s, qd_r, 3, range(4))
+    relay(qd, qd_s, qd_r, 0, 3)
+    relay(qd, qd_s, qd_r, 1, 3)
     key_grad([chip_at(step) for step in GROUPS[2]])
 
-    for n, (ref, factor) in enumerate(((dq, SCALE), (dk, SCALE), (dv, 1.0))):
-        swap[0, n] = (ref[...] * factor).astype(BF16)
-        send(swap.at[0, n, other_half], swap.at[1, n, 0:TOK], sib_s.at[7 + n], sib_r.at[7 + n], twin)
+    swap_send(1, dk, SCALE)
+    swap_send(2, dv, 1.0)
     arrived(gswap, sib_s.at[6], sib_r.at[6])
     gw_ref[0:HEAD, :] = jnp.where(c == 0, gf[0], gswap[...])
     gw_ref[HEAD : 2 * HEAD, :] = jnp.where(c == 0, gswap[...], gf[0])
@@ -425,6 +459,11 @@
         ref[:, HEAD : 2 * HEAD] = jnp.where(c == 0, other, own)
     for copy in sent:
         copy.wait_send()
+
+
+def copy_kernel(*refs):
+    for n in range(5):
+        refs[5 + n][...] = refs[n][...]
 
 
 def shards(queries, key_states, value_states, w_out, grad_y, chain_order):
@@ -447,18 +486,20 @@
         pltpu.VMEM((2, HEAD, HEAD), BF16),
         pltpu.VMEM((16, 8, CHIP), F32),
         pltpu.VMEM((CHIP, HEAD), BF16),
-        pltpu.VMEM((2, TOK, HEAD), BF16),
+        pltpu.VMEM((2, TOK, 2 * HEAD), BF16),
+        pltpu.VMEM((2, TOK, 2 * HEAD), BF16),
         pltpu.VMEM((2, 3, CHIP, HEAD), BF16),
         pltpu.VMEM((HEAD, HEAD), BF16),
     ]
     scratch += [pltpu.VMEM((CHIP, HEAD), F32)] * 6
-    scratch += [dma((N_COPIES,))] * 4
-    scratch += [dma((7,)), dma((10,)), dma((10,))]
+    scratch += [dma((2, N_COPIES))] * 4
+    scratch += [dma((2,)), dma((2,)), dma((12,)), dma((10,)), dma((10,))]
     scratch += [dma((7,))] * 4
-    scratch += [dma((6,))] * 2
-    scratch += [dma((8,))] * 2
+    scratch += [dma((2, 3))] * 2
+    scratch += [dma((2, 8))] * 2
+    scratch += [dma((4, 2))] * 2
     scratch += [dma((2, 3))] * 4
-    return pl.pallas_call(
+    results = pl.pallas_call(
         kernel,
         out_shape=(
             jax.ShapeDtypeStruct((TOK, 512), BF16),
@@ -475,6 +516,13 @@
         ),
         name="attention_layer",
     )(queries, key_states, value_states, w_out, grad_y, chain_order)
+    return pl.pallas_call(
+        copy_kernel,
+        out_shape=tuple(jax.ShapeDtypeStruct(r.shape, r.dtype) for r in results),
+        in_specs=[vmem] * 5,
+        out_specs=(vmem,) * 5,
+        name="results",
+    )(*results)
 
 
 def solution(mesh):

time: 85 us -> 71.6 us (0.84)
  local copies, waits for them, and re-layouts: 7.7 us -> 0 us
  Pallas kernels: 76.4 us -> 70.9 us
    unnamed x5 -> x0, local copies, waits for them, and re-layouts: 7.7 us -> none
    pallas_call x1, Pallas kernels: 76.4 us -> 69 us  [shards(): pl.pallas_call(kernel, out_shape=(jax.ShapeDtypeStruct((TOK, 512), BF16),...]
    pallas_call x0 -> x1, Pallas kernels: none -> 1.89 us  [shards(): pl.pallas_call(copy_kernel, out_shape=tuple((jax.ShapeDtypeStruct(r.shape...]
where the time goes in v2:
time: 71.6 us; the launch traced here: 71.5 us
  Pallas kernels  70.9 us (99%)
    pallas_call x1, Pallas kernels, shards(): pl.pallas_call(kernel, out_shape=(jax.ShapeDtypeStruct((TOK, 512), BF16),...  69 us
    pallas_call x1, Pallas kernels, shards(): pl.pallas_call(copy_kernel, out_shape=tuple((jax.ShapeDtypeStruct(r.shape...  1.89 us

profile of v2, /device:TPU:1, one launch (start us, length us, event | category | flops | bytes accessed | tf_op | source)
XLA Modules:
  0.0 71.5 jit_solution(12375818663712595789)
XLA Ops:
  0.6 69.0 %attention_layer.1 = (bf16[192,512]{1,0:T(8,128)(2,1)}, bf16[192,256]{1,0:T(8,128)(2,1)}, bf16[192,256]{1,0:T(8,128)(2,1)}, bf16[192,256]{1,0:T(8,128)(2,1)}, bf16[256,128]{1,0:T(8,128)(2,1)}) custom-call(bf16[192,256]{1,0:T(8,128)(2,1)} %q_hbm.1, bf16[192,256]{1,0:T(8,128)(2,1)} %k_hbm.1, bf16[192,256]{1,0:T(8,128)(2,1)} %v_hbm.1, bf16[256,4096]{1,0:T(8,128)(2,1)} %w_hbm.1, ...), custom_call_target="tpu_custom_call" | custom-call | tf_op jit(solution)/shard_map/attention_layer/pallas_call | solution.py:502
  69.7 1.9 %results.1 = (bf16[192,512]{1,0:T(8,128)(2,1)}, bf16[192,256]{1,0:T(8,128)(2,1)}, bf16[192,256]{1,0:T(8,128)(2,1)}, bf16[192,256]{1,0:T(8,128)(2,1)}, bf16[256,128]{1,0:T(8,128)(2,1)}) custom-call(bf16[192,512]{1,0:T(8,128)(2,1)} %get-tuple-element.10.refs_0_, bf16[192,256]{1,0:T(8,128)(2,1)} %get-tuple-element.11.refs_1_, ...), custom_call_target="tpu_custom_call" | custom-call | tf_op jit(solution)/shard_map/results/pallas_call | solution.py:519

commit v3 on v2

--- a/solution.py
+++ b/solution.py
@@ -69,6 +69,8 @@
 ]
 FIRST = [0, 4, 10, 16]
 N_COPIES = 18
+KV_SENT, QD_SENT, W_SENT, Z_SENT, TWIN_SENT, G_SENT, ST_SENT = range(7)
+N_GROUPS = 7
 GROUPS = [
     [(0, 0), (0, -1), (0, 1), (-1, 0), (1, 0)],
     [(0, 2), (2, 0), (-1, -1), (-1, 1), (1, -1), (1, 1)],
@@ -91,10 +93,9 @@
 def kernel(
     q_hbm, k_hbm, v_hbm, w_hbm, gy_hbm, order,
     out_ref, dq_ref, dk_ref, dv_ref, gw_ref,
-    kv, qd, wv, gyc, wc, ag, gb, r1, h1, r2, gf, st, attb, kvs, qds, swap, gswap,
+    kv, qd, wv, gyc, wc, ag, gb, ga, gt, gr, h1, ga2, gt2, gr2, st, attb, kvs, qds, swap, gswap,
     m, l, acc, dq, dk, dv,
-    kv_s, kv_r, qd_s, qd_r, own_s, own_r, loc, sib_s, sib_r, wz_s, wz_r, ws_s, ws_r, st_s, st_r,
-    az_s, az_r, a0_s, a0_r, g1_s, g1_r, g2_s, g2_r,
+    out_s, kv_r, qd_r, own_r, loc, sib_r, wz_r, ws_r, st_r, az_r, a0_r, g_r, gw_r,
 ):
     s = lax.axis_index("seq")
     z = lax.axis_index("head")
@@ -122,33 +123,38 @@
             src_ref=src, dst_ref=dst, send_sem=send, recv_sem=recv, device_id=device, device_id_type=MESH
         )
 
-    sent = []
-
-    def send(src, dst, ssem, rsem, device):
-        copy = remote(src, dst, ssem, rsem, device)
-        copy.start()
-        sent.append(copy)
-
-    def arrived(dst, ssem, rsem):
-        remote(dst, dst, ssem, rsem, twin).wait_recv()
+    totals = [0] * N_GROUPS
+
+    def send(src, dst, group, rsem, device):
+        remote(src, dst, out_s.at[group], rsem, device).start()
+        totals[group] += math.prod(src.shape)
+
+    def all_sent():
+        for group, total in enumerate(totals):
+            if group == ST_SENT:
+                place = st.at[0 : total // (8 * CHIP)]
+            else:
+                place = kv.at[0 : total // (2 * HEAD)]
+            remote(place, place, out_s.at[group], out_s.at[group], twin).wait_send()
+
+    def arrived(dst, rsem):
+        remote(dst, dst, rsem, rsem, twin).wait_recv()
 
     def same(a, b):
         return (a[0] - b[0]) % 4 == 0 and (a[1] - b[1]) % 4 == 0
 
-    def hop_send(buf, ssem, rsem, flow, hop, step=None):
+    def hop_send(buf, group, rsem, flow, hop, step):
         for i, (source, part, way) in enumerate(FLOWS[flow][hop]):
-            if step is None or same(step, source):
+            if same(step, source):
                 place = buf.at[rows(source, part)]
-                n = FIRST[hop] + i
-                send(place, place, ssem.at[flow, n], rsem.at[flow, n], at(way))
-
-    def relay(buf, ssem, rsem, flow, hop):
+                send(place, place, group, rsem.at[flow, FIRST[hop] + i], at(way))
+
+    def relay(buf, group, rsem, flow, hop):
         for i, (source, part, way) in enumerate(FLOWS[flow][hop]):
             step = (source[0] - way[0], source[1] - way[1])
-            n = FIRST[hop] + i
-            arrived(buf.at[rows(step, part)], ssem.at[flow, n], rsem.at[flow, n])
+            arrived(buf.at[rows(step, part)], rsem.at[flow, FIRST[hop] + i])
             if hop < 3:
-                hop_send(buf, ssem, rsem, flow, hop + 1, step)
+                hop_send(buf, group, rsem, flow, hop + 1, step)
 
     mine = pl.ds(pl.multiple_of(s * TOK, 32), TOK)
     half = pl.ds(pl.multiple_of(c * TOK, 32), TOK)
@@ -183,25 +189,28 @@
         pl.semaphore_signal(barrier, inc=1, device_id=peer, device_id_type=MESH)
     pl.semaphore_wait(barrier, len(peers))
 
-    def first_send(buf, stage, which, ssem, rsem):
+    def first_send(buf, stage, group, rsem):
         for i, way in enumerate((RIGHT, LEFT, DOWN, UP)):
             for h in range(2):
-                send(stage.at[h], buf.at[mine], ssem.at[h, i], rsem.at[c, i], (chip_at(way) * 2 + h, z))
-        send(stage.at[o], buf.at[mine], own_s.at[which], own_r.at[which], twin)
-        own = pltpu.make_async_copy(stage.at[c], buf.at[mine], loc.at[9 + which])
+                send(stage.at[h], buf.at[mine], group, rsem.at[c, i], (chip_at(way) * 2 + h, z))
+
+    def own_send(buf, stage, group):
+        send(stage.at[o], buf.at[mine], group, own_r.at[group], twin)
+        own = pltpu.make_async_copy(stage.at[c], buf.at[mine], loc.at[9 + group])
         own.start()
         return own
 
     theirs = pl.ds(pl.multiple_of((s + 1 - 2 * c) * TOK, 32), TOK)
     for n in (0, 1, 3, 4):
         local[n].wait()
-    own_kv = first_send(kv, kvs, 0, kv_s, kv_r)
+    first_send(kv, kvs, KV_SENT, kv_r)
+    own_kv = own_send(kv, kvs, KV_SENT)
     for d in range(1, N_Z):
         far = wrap(z + d, N_Z)
         send(
-            w_hbm.at[cols(c), cols(far, 512)], wc.at[z, cols(c)], wz_s.at[d - 1], wz_r.at[d - 1], (s, far)
+            w_hbm.at[cols(c), cols(far, 512)], wc.at[z, cols(c)], W_SENT, wz_r.at[d - 1], (s, far)
         )
-    send(gy_hbm, gyc.at[half], sib_s.at[4], sib_r.at[4], twin)
+    send(gy_hbm, gyc.at[half], TWIN_SENT, sib_r.at[4], twin)
 
     local[6].wait()
     local[7].wait()
@@ -261,14 +270,14 @@
             dscore = (probs * (slopes - l[rs, 0:1])).astype(BF16)
             dq[rs, :] += dot(dscore, keys)
 
-    def key_grad(chips):
+    def key_grad(chips, halves=(0, 1)):
         queries = jnp.concatenate([qd[chip_rows(n), 0:HEAD] for n in chips], axis=0)
         douts = jnp.concatenate([qd[chip_rows(n), HEAD : 2 * HEAD] for n in chips], axis=0)
         query_pos = row_pos(chips)
         norm = jnp.concatenate([st[n, 0:1, :] for n in chips], axis=1)
         delta = jnp.concatenate([st[n, 1:2, :] for n in chips], axis=1)
-        for a in range(2):
-            rs = slice(a * TOK, (a + 1) * TOK)
+        for a in halves:
+            rs = slice(a * TOK, (a + 1) * TOK) if isinstance(a, int) else pl.ds(pl.multiple_of(a * TOK, 32), TOK)
             scores = dot_nt(kv[own_rows(a), 0:HEAD], queries) * SCALE2 - norm
             probs = jnp.exp2(jnp.where(col_pos(a) <= query_pos, scores, NEG))
             dv[rs, :] += dot(probs.astype(BF16), douts)
@@ -276,26 +285,27 @@
             dscore = (probs * (slopes - delta)).astype(BF16)
             dk[rs, :] += dot(dscore, queries)
 
-    relay(kv, kv_s, kv_r, 0, 0)
-    relay(kv, kv_s, kv_r, 1, 0)
+    relay(kv, KV_SENT, kv_r, 0, 0)
+    relay(kv, KV_SENT, kv_r, 1, 0)
     own_kv.wait()
-    arrived(kv.at[theirs], own_s.at[0], own_r.at[0])
-    own_qd = first_send(qd, qds, 1, qd_s, qd_r)
+    arrived(kv.at[theirs], own_r.at[0])
+    own_qd = own_send(qd, qds, QD_SENT)
     own_qd.wait()
-    arrived(qd.at[theirs], own_s.at[1], own_r.at[1])
+    arrived(qd.at[theirs], own_r.at[1])
     forward([chip_at(step) for step in GROUPS[0]])
 
-    relay(kv, kv_s, kv_r, 0, 1)
-    relay(kv, kv_s, kv_r, 1, 1)
+    relay(kv, KV_SENT, kv_r, 0, 1)
+    relay(kv, KV_SENT, kv_r, 1, 1)
+    first_send(qd, qds, QD_SENT, qd_r)
     forward([chip_at(step) for step in GROUPS[1]])
 
-    relay(kv, kv_s, kv_r, 0, 2)
-    relay(kv, kv_s, kv_r, 1, 2)
-    relay(qd, qd_s, qd_r, 0, 0)
-    relay(qd, qd_s, qd_r, 1, 0)
+    relay(kv, KV_SENT, kv_r, 0, 2)
+    relay(kv, KV_SENT, kv_r, 1, 2)
+    relay(qd, QD_SENT, qd_r, 0, 0)
+    relay(qd, QD_SENT, qd_r, 1, 0)
     forward([chip_at(step) for step in GROUPS[2][:4]])
-    relay(kv, kv_s, kv_r, 0, 3)
-    relay(kv, kv_s, kv_r, 1, 3)
+    relay(kv, KV_SENT, kv_r, 0, 3)
+    relay(kv, KV_SENT, kv_r, 1, 3)
     forward([chip_at(step) for step in GROUPS[2][4:]])
 
     for a in range(2):
@@ -311,7 +321,7 @@
     st[chip] = jnp.transpose(jnp.where(lane == 0, m[...], l[...]))[0:8, :]
 
     for d in (1, 2, 3):
-        send(st.at[chip], st.at[chip], st_s.at[0, d - 1], st_r.at[0, d - 1], at((0, d)))
+        send(st.at[chip], st.at[chip], ST_SENT, st_r.at[0, d - 1], at((0, d)))
     own_att = pltpu.make_async_copy(attb.at[half], ag.at[z, :, cols(c)], loc.at[11])
     own_att.start()
     for part in range(2):
@@ -320,19 +330,20 @@
                 send(
                     attb.at[h * TOK + part * HALF : h * TOK + (part + 1) * HALF],
                     ag.at[z, part * HALF : (part + 1) * HALF, cols(c)],
-                    a0_s.at[2 * n + part, h],
+                    Z_SENT,
                     a0_r.at[2 * n + part, c],
                     (chip * 2 + h, wrap(z + step, N_Z)),
                 )
-    send(attb.at[other_half], ag.at[z, :, cols(c)], sib_s.at[5], sib_r.at[5], twin)
-
-    arrived(gyc.at[other_half], sib_s.at[4], sib_r.at[4])
+    send(attb.at[other_half], ag.at[z, :, cols(c)], TWIN_SENT, sib_r.at[5], twin)
+
+    arrived(gyc.at[other_half], sib_r.at[4])
     att_t = jnp.transpose(attb[...].astype(F32)).astype(BF16)
 
-    @pl.loop(0, 16)
+    @pl.loop(0, 4)
     def _(n):
-        part = dot(att_t, gyc[:, pl.ds(pl.multiple_of(n * 256, 256), 256)])
-        gb[n // 4, lax.rem(n, 4)] = part.astype(BF16)
+        part = dot(att_t, gyc[:, pl.ds(pl.multiple_of(n * 1024, 1024), 1024)]).astype(BF16)
+        for i in range(4):
+            gb[n, i] = part[:, i * 256 : (i + 1) * 256]
 
 
     def z_at(step):
@@ -344,7 +355,7 @@
     def z_send(hop, way, part):
         place = z_place(-way * hop, part)
         n = way_index(way), 2 * hop + part
-        send(place, place, az_s.at[n], az_r.at[n], (s, z_at(way)))
+        send(place, place, Z_SENT, az_r.at[n], (s, z_at(way)))
 
     def way_index(way):
         return 0 if way > 0 else 1
@@ -358,107 +369,140 @@
                 if hop == 0:
                     for h in range(2):
                         place = ag.at[z_at(-way), part * HALF : (part + 1) * HALF, cols(h)]
-                        arrived(place, a0_s.at[2 * n[0] + part, h], a0_r.at[2 * n[0] + part, h])
+                        arrived(place, a0_r.at[2 * n[0] + part, h])
                 else:
-                    arrived(z_place(-way * (hop + 1), part), az_s.at[n], az_r.at[n])
+                    arrived(z_place(-way * (hop + 1), part), az_r.at[n])
                 if hop < 2 or (hop == 2 and part == way_index(way)):
                     z_send(hop + 1, way, part)
 
-    upper, lower = slice(0, 64), slice(64, 128)
-    for d in (1, 2, 3):
-        send(gb.at[:, wrap(x + d, 4), upper], r1.at[0, d - 1], g1_s.at[0, d - 1], g1_r.at[0, d - 1], at((0, d)))
-        send(gb.at[wrap(y + d, 4), :, lower], r1.at[1, d - 1], g1_s.at[1, d - 1], g1_r.at[1, d - 1], at((d, 0)))
+    def axis_at(way, stage, d):
+        return at((0, d)) if way == stage else at((d, 0))
+
+    def slab(way, d, first, size):
+        span = pl.ds(way * 64 + first, size)
+        return gb.at[:, wrap(x + d, 4), span] if way == 0 else gb.at[wrap(y + d, 4), :, span]
+
+    def second(way, d):
+        return wrap((y if way == 0 else x) + d, 4)
+
+    def added(first, *others):
+        total = first.astype(F32)
+        for other in others:
+            total = total + other.astype(F32)
+        return total
+
+    def sum_far():
+        for way in range(2):
+            for n, d in enumerate((1, -1)):
+                send(slab(way, 2, 32 * n, 32), ga.at[way, n], G_SENT, g_r.at[way, n], axis_at(way, 0, d))
+
+    def sum_near():
+        for way in range(2):
+            for n, d in enumerate((1, -1)):
+                arrived(ga.at[way, n], g_r.at[way, n])
+                rest = slice(32 - 32 * n, 64 - 32 * n)
+                gt[way, n, :, 32 * n : 32 * n + 32] = added(slab(way, d, 32 * n, 32)[...], ga[way, n]).astype(BF16)
+                gt[way, n, :, rest] = slab(way, d, 32 - 32 * n, 32)[...]
+                send(gt.at[way, n], gr.at[way, n], G_SENT, g_r.at[2 + way, n], axis_at(way, 0, d))
+
+    def sum_far_again():
+        for way in range(2):
+            for n in range(2):
+                arrived(gr.at[way, n], g_r.at[2 + way, n])
+            h1[way] = added(slab(way, 0, 0, 64)[...], gr[way, 0], gr[way, 1]).astype(BF16)
+            for n, d in enumerate((1, -1)):
+                place = h1.at[way, second(way, 2), pl.ds(32 * n, 32)]
+                send(place, ga2.at[way, n], G_SENT, g_r.at[4 + way, n], axis_at(way, 1, d))
+            send(h1.at[way, second(way, 0), :, cols(o)], gswap.at[way], G_SENT, sib_r.at[way], twin)
+
+    def sum_near_again():
+        for way in range(2):
+            for n, d in enumerate((1, -1)):
+                arrived(ga2.at[way, n], g_r.at[4 + way, n])
+                block = h1[way, second(way, d)]
+                rest = slice(32 - 32 * n, 64 - 32 * n)
+                gt2[way, n, 32 * n : 32 * n + 32] = added(block[32 * n : 32 * n + 32], ga2[way, n]).astype(BF16)
+                gt2[way, n, rest] = block[rest]
+                for h in range(2):
+                    device = axis_at(way, 1, d)
+                    device = (device[0] - c + h, z)
+                    send(gt2.at[way, n, :, cols(h)], gr2.at[way, n, c], G_SENT, gw_r.at[2 * way + n, c], device)
+
+    def sum_last():
+        for way in range(2):
+            arrived(gswap.at[way], sib_r.at[way])
+            own = h1[way, second(way, 0)]
+            own = jnp.where(c == 0, own[:, 0:HEAD], own[:, HEAD:])
+            for h in range(2):
+                for n in range(2):
+                    arrived(gr2.at[way, n, h], gw_r.at[2 * way + n, h])
+                total = added(jnp.where(c == h, own, gswap[way]), gr2[way, 0, h], gr2[way, 1, h])
+                gw_ref[h * HEAD + way * 64 : h * HEAD + way * 64 + 64, :] = total.astype(BF16)
+
+    sum_far()
 
     def st_row(step):
         return st.at[pl.ds(wrap(y + step, 4) * 4, 4)]
 
     def swap_send(n, ref, factor):
-        swap[0, n] = (ref[...] * factor).astype(BF16)
-        send(swap.at[0, n, other_half], swap.at[1, n, 0:TOK], sib_s.at[7 + n], sib_r.at[7 + n], twin)
-
-    relay(qd, qd_s, qd_r, 0, 1)
-    relay(qd, qd_s, qd_r, 1, 1)
+        swap[0, n] = (ref[other_half, :] * factor).astype(BF16)
+        send(swap.at[0, n], swap.at[1, n], TWIN_SENT, sib_r.at[7 + n], twin)
+
+    query_grad(list(range(0, 4)))
+    relay(qd, QD_SENT, qd_r, 0, 1)
+    relay(qd, QD_SENT, qd_r, 1, 1)
     z_relay(0)
     for d in (1, 2, 3):
-        arrived(st.at[chip_at((0, -d))], st_s.at[0, d - 1], st_r.at[0, d - 1])
+        arrived(st.at[chip_at((0, -d))], st_r.at[0, d - 1])
     for d in (1, 2, 3):
-        send(st_row(0), st_row(0), st_s.at[1, d - 1], st_r.at[1, d - 1], at((d, 0)))
-    query_grad(list(range(0, 4)))
+        send(st_row(0), st_row(0), ST_SENT, st_r.at[1, d - 1], at((d, 0)))
     query_grad(list(range(4, 8)))
+    sum_near()
     z_relay(1)
     for d in range(1, N_Z):
         place = wc.at[z_at(-d), cols(c)]
-        arrived(place, wz_s.at[d - 1], wz_r.at[d - 1])
-        send(place, place, ws_s.at[d - 1], ws_r.at[d - 1], twin)
+        arrived(place, wz_r.at[d - 1])
+        send(place, place, W_SENT, ws_r.at[d - 1], twin)
     query_grad(list(range(8, 12)))
-    relay(qd, qd_s, qd_r, 0, 2)
-    relay(qd, qd_s, qd_r, 1, 2)
+    relay(qd, QD_SENT, qd_r, 0, 2)
+    relay(qd, QD_SENT, qd_r, 1, 2)
     z_relay(2)
     query_grad(list(range(12, 16)))
+    sum_far_again()
+    swap_send(0, dq, SCALE)
     for d in (1, 2, 3):
-        arrived(st_row(-d), st_s.at[1, d - 1], st_r.at[1, d - 1])
-    swap_send(0, dq, SCALE)
-
-    for way in range(2):
-        for d in (1, 2, 3):
-            arrived(r1.at[way, d - 1], g1_s.at[way, d - 1], g1_r.at[way, d - 1])
-    for n in range(4):
-        total = gb[n, x, upper].astype(F32)
-        for d in range(3):
-            total = total + r1[0, d, n].astype(F32)
-        h1[0, n] = total.astype(BF16)
-        total = gb[y, n, lower].astype(F32)
-        for d in range(3):
-            total = total + r1[1, d, n].astype(F32)
-        h1[1, n] = total.astype(BF16)
-    for d in (1, 2, 3):
-        send(h1.at[0, wrap(y + d, 4)], r2.at[0, d - 1], g2_s.at[0, d - 1], g2_r.at[0, d - 1], at((d, 0)))
-        send(h1.at[1, wrap(x + d, 4)], r2.at[1, d - 1], g2_s.at[1, d - 1], g2_r.at[1, d - 1], at((0, d)))
-
+        arrived(st_row(-d), st_r.at[1, d - 1])
     key_grad([chip_at(step) for step in GROUPS[0]])
+    sum_near_again()
     key_grad([chip_at(step) for step in GROUPS[1]])
 
-    for way in range(2):
-        for d in (1, 2, 3):
-            arrived(r2.at[way, d - 1], g2_s.at[way, d - 1], g2_r.at[way, d - 1])
-    for way, own in ((0, y), (1, x)):
-        total = h1[way, own].astype(F32)
-        for d in range(3):
-            total = total + r2[way, d].astype(F32)
-        total = total.astype(BF16)
-        rs = slice(way * 64, way * 64 + 64)
-        gf[0, rs, :] = jnp.where(c == 0, total[:, 0:HEAD], total[:, HEAD:])
-        gf[1, rs, :] = jnp.where(c == 0, total[:, HEAD:], total[:, 0:HEAD])
-    send(gf.at[1], gswap, sib_s.at[6], sib_r.at[6], twin)
-
     for d in range(1, N_Z):
-        arrived(wc.at[z_at(-d), cols(o)], ws_s.at[d - 1], ws_r.at[d - 1])
+        arrived(wc.at[z_at(-d), cols(o)], ws_r.at[d - 1])
     z_relay(3)
     local[8].wait()
     own_att.wait()
-    arrived(ag.at[z, :, cols(o)], sib_s.at[5], sib_r.at[5])
+    arrived(ag.at[z, :, cols(o)], sib_r.at[5])
     total = dot(ag[0], wc[0])
     for n in range(1, N_Z):
         total = total + dot(ag[n], wc[n])
     out_ref[...] = total.astype(BF16)
-
-    relay(qd, qd_s, qd_r, 0, 3)
-    relay(qd, qd_s, qd_r, 1, 3)
-    key_grad([chip_at(step) for step in GROUPS[2]])
-
+    sum_last()
+
+    key_grad([chip_at(step) for step in GROUPS[2][:4]])
+    relay(qd, QD_SENT, qd_r, 0, 3)
+    relay(qd, QD_SENT, qd_r, 1, 3)
+    key_grad([chip_at(step) for step in GROUPS[2][4:]], (o,))
     swap_send(1, dk, SCALE)
     swap_send(2, dv, 1.0)
-    arrived(gswap, sib_s.at[6], sib_r.at[6])
-    gw_ref[0:HEAD, :] = jnp.where(c == 0, gf[0], gswap[...])
-    gw_ref[HEAD : 2 * HEAD, :] = jnp.where(c == 0, gswap[...], gf[0])
-    for n, ref in enumerate((dq_ref, dk_ref, dv_ref)):
-        arrived(swap.at[1, n, 0:TOK], sib_s.at[7 + n], sib_r.at[7 + n])
-        own = swap[0, n, half, :]
-        other = swap[1, n, 0:TOK, :]
+    key_grad([chip_at(step) for step in GROUPS[2][4:]], (c,))
+
+    for n, (ref, total, factor) in enumerate(((dq_ref, dq, SCALE), (dk_ref, dk, SCALE), (dv_ref, dv, 1.0))):
+        own = (total[half, :] * factor).astype(BF16)
+        arrived(swap.at[1, n], sib_r.at[7 + n])
+        other = swap[1, n]
         ref[:, 0:HEAD] = jnp.where(c == 0, own, other)
         ref[:, HEAD : 2 * HEAD] = jnp.where(c == 0, other, own)
-    for copy in sent:
-        copy.wait_send()
+    all_sent()
 
 
 def copy_kernel(*refs):
@@ -480,25 +524,23 @@
         pltpu.VMEM((N_Z, 2 * HEAD, 512), BF16),
         pltpu.VMEM((N_Z, TOK, 2 * HEAD), BF16),
         pltpu.VMEM((4, 4, HEAD, 256), BF16),
-        pltpu.VMEM((2, 3, 4, 64, 256), BF16),
+        pltpu.VMEM((2, 2, 4, 32, 256), BF16),
+        pltpu.VMEM((2, 2, 4, 64, 256), BF16),
+        pltpu.VMEM((2, 2, 4, 64, 256), BF16),
         pltpu.VMEM((2, 4, 64, 256), BF16),
-        pltpu.VMEM((2, 3, 64, 256), BF16),
-        pltpu.VMEM((2, HEAD, HEAD), BF16),
+        pltpu.VMEM((2, 2, 32, 256), BF16),
+        pltpu.VMEM((2, 2, 64, 256), BF16),
+        pltpu.VMEM((2, 2, 2, 64, HEAD), BF16),
         pltpu.VMEM((16, 8, CHIP), F32),
         pltpu.VMEM((CHIP, HEAD), BF16),
         pltpu.VMEM((2, TOK, 2 * HEAD), BF16),
         pltpu.VMEM((2, TOK, 2 * HEAD), BF16),
-        pltpu.VMEM((2, 3, CHIP, HEAD), BF16),
-        pltpu.VMEM((HEAD, HEAD), BF16),
+        pltpu.VMEM((2, 3, TOK, HEAD), BF16),
+        pltpu.VMEM((2, 64, HEAD), BF16),
     ]
     scratch += [pltpu.VMEM((CHIP, HEAD), F32)] * 6
-    scratch += [dma((2, N_COPIES))] * 4
-    scratch += [dma((2,)), dma((2,)), dma((12,)), dma((10,)), dma((10,))]
-    scratch += [dma((7,))] * 4
-    scratch += [dma((2, 3))] * 2
-    scratch += [dma((2, 8))] * 2
-    scratch += [dma((4, 2))] * 2
-    scratch += [dma((2, 3))] * 4
+    scratch += [dma((N_GROUPS,)), dma((2, N_COPIES)), dma((2, N_COPIES)), dma((2,)), dma((12,)), dma((10,))]
+    scratch += [dma((7,)), dma((7,)), dma((2, 3)), dma((2, 8)), dma((4, 2)), dma((6, 2)), dma((4, 2))]
     results = pl.pallas_call(
         kernel,
         out_shape=(

time: 71.6 us -> 69 us (0.964)
  Pallas kernels: 70.9 us -> 68.2 us
    pallas_call x1, Pallas kernels: 69 us -> 66.3 us  [shards(): pl.pallas_call(kernel, out_shape=(jax.ShapeDtypeStruct((TOK, 512), BF16),...]
where the time goes in v3:
time: 69 us; the launch traced here: 68.9 us
  Pallas kernels  68.2 us (99%)
    pallas_call x1, Pallas kernels, shards(): pl.pallas_call(kernel, out_shape=(jax.ShapeDtypeStruct((TOK, 512), BF16),...  66.3 us
    pallas_call x1, Pallas kernels, shards(): pl.pallas_call(copy_kernel, out_shape=tuple((jax.ShapeDtypeStruct(r.shape...  1.89 us

profile of v3, /device:TPU:1, one launch (start us, length us, event | category | flops | bytes accessed | tf_op | source)
XLA Modules:
  0.0 68.9 jit_solution(6493368707034521921)
XLA Ops:
  0.6 66.3 %attention_layer.1 = (bf16[192,512]{1,0:T(8,128)(2,1)}, bf16[192,256]{1,0:T(8,128)(2,1)}, bf16[192,256]{1,0:T(8,128)(2,1)}, bf16[192,256]{1,0:T(8,128)(2,1)}, bf16[256,128]{1,0:T(8,128)(2,1)}) custom-call(bf16[192,256]{1,0:T(8,128)(2,1)} %q_hbm.1, bf16[192,256]{1,0:T(8,128)(2,1)} %k_hbm.1, bf16[192,256]{1,0:T(8,128)(2,1)} %v_hbm.1, bf16[256,4096]{1,0:T(8,128)(2,1)} %w_hbm.1, ...), custom_call_target="tpu_custom_call" | custom-call | tf_op jit(solution)/shard_map/attention_layer/pallas_call | solution.py:544
  67.0 1.9 %results.1 = (bf16[192,512]{1,0:T(8,128)(2,1)}, bf16[192,256]{1,0:T(8,128)(2,1)}, bf16[192,256]{1,0:T(8,128)(2,1)}, bf16[192,256]{1,0:T(8,128)(2,1)}, bf16[256,128]{1,0:T(8,128)(2,1)}) custom-call(bf16[192,512]{1,0:T(8,128)(2,1)} %get-tuple-element.10.refs_0_, bf16[192,256]{1,0:T(8,128)(2,1)} %get-tuple-element.11.refs_1_, ...), custom_call_target="tpu_custom_call" | custom-call | tf_op jit(solution)/shard_map/results/pallas_call | solution.py:561

commit v4 on v3

--- a/solution.py
+++ b/solution.py
@@ -94,7 +94,7 @@
     q_hbm, k_hbm, v_hbm, w_hbm, gy_hbm, order,
     out_ref, dq_ref, dk_ref, dv_ref, gw_ref,
     kv, qd, wv, gyc, wc, ag, gb, ga, gt, gr, h1, ga2, gt2, gr2, st, attb, kvs, qds, swap, gswap,
-    m, l, acc, dq, dk, dv,
+    m, l, ds, dl, dq, dk, dv, acc,
     out_s, kv_r, qd_r, own_r, loc, sib_r, wz_r, ws_r, st_r, az_r, a0_r, g_r, gw_r,
 ):
     s = lax.axis_index("seq")
@@ -174,7 +174,7 @@
     for copy in local:
         copy.start()
     m[...] = jnp.full_like(m, NEG)
-    for ref in (l, acc, dq, dk, dv):
+    for ref in (l, ds, dl, dq, dk, dv, acc):
         ref[...] = jnp.zeros_like(ref)
 
     barrier = pltpu.get_barrier_semaphore()
@@ -239,9 +239,15 @@
     def chip_rows(n):
         return pl.ds(pl.multiple_of(n * CHIP, 128), CHIP)
 
+    def lanes(wide):
+        total = wide[:, 0:HEAD]
+        for t in range(1, wide.shape[1] // HEAD):
+            total = total + wide[:, t * HEAD : (t + 1) * HEAD]
+        return total
+
     def forward(chips):
-        keys = jnp.concatenate([kv[chip_rows(n), 0:HEAD] for n in chips], axis=0)
-        values = jnp.concatenate([kv[chip_rows(n), HEAD : 2 * HEAD] for n in chips], axis=0)
+        blocks = jnp.concatenate([kv[chip_rows(n), :] for n in chips], axis=0)
+        keys, values = blocks[:, 0:HEAD], blocks[:, HEAD:]
         key_pos = row_pos(chips)
         for a in range(2):
             rs = slice(a * TOK, (a + 1) * TOK)
@@ -252,23 +258,18 @@
             factor = jnp.exp2(before - now)
             weights = jnp.exp2(scores - now)
             m[rs, :] = jnp.broadcast_to(now, (TOK, HEAD))
-            total = weights[:, 0:HEAD]
-            for t in range(1, weights.shape[1] // HEAD):
-                total = total + weights[:, t * HEAD : (t + 1) * HEAD]
-            l[rs, :] = l[rs, :] * factor + total
-            acc[rs, :] = acc[rs, :] * factor + dot(weights.astype(BF16), values)
-
-    def query_grad(chips):
-        keys = jnp.concatenate([kv[chip_rows(n), 0:HEAD] for n in chips], axis=0)
-        values = jnp.concatenate([kv[chip_rows(n), HEAD : 2 * HEAD] for n in chips], axis=0)
-        key_pos = row_pos(chips)
-        for a in range(2):
-            rs = slice(a * TOK, (a + 1) * TOK)
-            scores = dot_nt(qd[own_rows(a), 0:HEAD], keys) * SCALE2 - m[rs, 0:1]
-            probs = jnp.exp2(jnp.where(key_pos <= col_pos(a), scores, NEG))
             slopes = dot_nt(qd[own_rows(a), HEAD : 2 * HEAD], values)
-            dscore = (probs * (slopes - l[rs, 0:1])).astype(BF16)
-            dq[rs, :] += dot(dscore, keys)
+            norms = l[rs, :] * factor + lanes(weights)
+            deltas = ds[rs, :] * factor + lanes(weights * slopes)
+            l[rs, :] = norms
+            ds[rs, :] = deltas
+            delta = jnp.sum(deltas, axis=1, keepdims=True) / jnp.sum(norms, axis=1, keepdims=True)
+            moved = delta - dl[rs, 0:1]
+            dl[rs, :] = jnp.broadcast_to(delta, (TOK, HEAD))
+            old = acc[rs, :] * factor
+            dscore = (weights * (slopes - delta)).astype(BF16)
+            dq[rs, :] = dq[rs, :] * factor - moved * old[:, 0:HEAD] + dot(dscore, keys)
+            acc[rs, :] = old + dot(weights.astype(BF16), blocks)
 
     def key_grad(chips, halves=(0, 1)):
         queries = jnp.concatenate([qd[chip_rows(n), 0:HEAD] for n in chips], axis=0)
@@ -311,10 +312,11 @@
     for a in range(2):
         rs = slice(a * TOK, (a + 1) * TOK)
         denominator = jnp.sum(l[rs, :], axis=1, keepdims=True)
-        attention = (acc[rs, :] / denominator).astype(BF16)
+        attention = (acc[rs, HEAD:] / denominator).astype(BF16)
         attb[rs, :] = attention
         grads = qd[own_rows(a), HEAD : 2 * HEAD].astype(F32)
         delta = jnp.sum(grads * attention.astype(F32), axis=1, keepdims=True)
+        dq[rs, :] = (dq[rs, :] - (delta - dl[rs, 0:1]) * acc[rs, 0:HEAD]) / denominator
         m[rs, :] = jnp.broadcast_to(m[rs, 0:1] + jnp.log2(denominator), (TOK, HEAD))
         l[rs, :] = jnp.broadcast_to(delta, (TOK, HEAD))
     lane = lax.broadcasted_iota(jnp.int32, (CHIP, HEAD), 1)
@@ -448,33 +450,37 @@
         swap[0, n] = (ref[other_half, :] * factor).astype(BF16)
         send(swap.at[0, n], swap.at[1, n], TWIN_SENT, sib_r.at[7 + n], twin)
 
-    query_grad(list(range(0, 4)))
+    swap_send(0, dq, SCALE)
     relay(qd, QD_SENT, qd_r, 0, 1)
     relay(qd, QD_SENT, qd_r, 1, 1)
-    z_relay(0)
     for d in (1, 2, 3):
         arrived(st.at[chip_at((0, -d))], st_r.at[0, d - 1])
     for d in (1, 2, 3):
         send(st_row(0), st_row(0), ST_SENT, st_r.at[1, d - 1], at((d, 0)))
-    query_grad(list(range(4, 8)))
+    z_relay(0)
     sum_near()
-    z_relay(1)
     for d in range(1, N_Z):
         place = wc.at[z_at(-d), cols(c)]
         arrived(place, wz_r.at[d - 1])
         send(place, place, W_SENT, ws_r.at[d - 1], twin)
-    query_grad(list(range(8, 12)))
-    relay(qd, QD_SENT, qd_r, 0, 2)
-    relay(qd, QD_SENT, qd_r, 1, 2)
-    z_relay(2)
-    query_grad(list(range(12, 16)))
-    sum_far_again()
-    swap_send(0, dq, SCALE)
     for d in (1, 2, 3):
         arrived(st_row(-d), st_r.at[1, d - 1])
     key_grad([chip_at(step) for step in GROUPS[0]])
+    z_relay(1)
+    relay(qd, QD_SENT, qd_r, 0, 2)
+    relay(qd, QD_SENT, qd_r, 1, 2)
+    sum_far_again()
+    key_grad([chip_at(step) for step in GROUPS[1]])
+    z_relay(2)
     sum_near_again()
-    key_grad([chip_at(step) for step in GROUPS[1]])
+    key_grad([chip_at(step) for step in GROUPS[2][:4]])
+
+    relay(qd, QD_SENT, qd_r, 0, 3)
+    relay(qd, QD_SENT, qd_r, 1, 3)
+    key_grad([chip_at(step) for step in GROUPS[2][4:]], (o,))
+    swap_send(1, dk, SCALE)
+    swap_send(2, dv, 1.0)
+    key_grad([chip_at(step) for step in GROUPS[2][4:]], (c,))
 
     for d in range(1, N_Z):
         arrived(wc.at[z_at(-d), cols(o)], ws_r.at[d - 1])
@@ -487,14 +493,6 @@
         total = total + dot(ag[n], wc[n])
     out_ref[...] = total.astype(BF16)
     sum_last()
-
-    key_grad([chip_at(step) for step in GROUPS[2][:4]])
-    relay(qd, QD_SENT, qd_r, 0, 3)
-    relay(qd, QD_SENT, qd_r, 1, 3)
-    key_grad([chip_at(step) for step in GROUPS[2][4:]], (o,))
-    swap_send(1, dk, SCALE)
-    swap_send(2, dv, 1.0)
-    key_grad([chip_at(step) for step in GROUPS[2][4:]], (c,))
 
     for n, (ref, total, factor) in enumerate(((dq_ref, dq, SCALE), (dk_ref, dk, SCALE), (dv_ref, dv, 1.0))):
         own = (total[half, :] * factor).astype(BF16)
@@ -538,7 +536,8 @@
         pltpu.VMEM((2, 3, TOK, HEAD), BF16),
         pltpu.VMEM((2, 64, HEAD), BF16),
     ]
-    scratch += [pltpu.VMEM((CHIP, HEAD), F32)] * 6
+    scratch += [pltpu.VMEM((CHIP, HEAD), F32)] * 7
+    scratch += [pltpu.VMEM((CHIP, 2 * HEAD), F32)]
     scratch += [dma((N_GROUPS,)), dma((2, N_COPIES)), dma((2, N_COPIES)), dma((2,)), dma((12,)), dma((10,))]
     scratch += [dma((7,)), dma((7,)), dma((2, 3)), dma((2, 8)), dma((4, 2)), dma((6, 2)), dma((4, 2))]
     results = pl.pallas_call(

time: 69 us -> 66.8 us (0.968)
  Pallas kernels: 68.2 us -> 66 us
    pallas_call x1, Pallas kernels: 66.3 us -> 64.2 us  [shards(): pl.pallas_call(kernel, out_shape=(jax.ShapeDtypeStruct((TOK, 512), BF16),...]
where the time goes in v4:
time: 66.8 us; the launch traced here: 66.7 us
  Pallas kernels  66 us (99%)
    pallas_call x1, Pallas kernels, shards(): pl.pallas_call(kernel, out_shape=(jax.ShapeDtypeStruct((TOK, 512), BF16),...  64.2 us
    pallas_call x1, Pallas kernels, shards(): pl.pallas_call(copy_kernel, out_shape=tuple((jax.ShapeDtypeStruct(r.shape...  1.89 us

profile of v4, /device:TPU:1, one launch (start us, length us, event | category | flops | bytes accessed | tf_op | source)
XLA Modules:
  0.0 66.7 jit_solution(3012472037821663685)
XLA Ops:
  0.6 64.2 %attention_layer.1 = (bf16[192,512]{1,0:T(8,128)(2,1)}, bf16[192,256]{1,0:T(8,128)(2,1)}, bf16[192,256]{1,0:T(8,128)(2,1)}, bf16[192,256]{1,0:T(8,128)(2,1)}, bf16[256,128]{1,0:T(8,128)(2,1)}) custom-call(bf16[192,256]{1,0:T(8,128)(2,1)} %q_hbm.1, bf16[192,256]{1,0:T(8,128)(2,1)} %k_hbm.1, bf16[192,256]{1,0:T(8,128)(2,1)} %v_hbm.1, bf16[256,4096]{1,0:T(8,128)(2,1)} %w_hbm.1, ...), custom_call_target="tpu_custom_call" | custom-call | tf_op jit(solution)/shard_map/attention_layer/pallas_call | solution.py:543
  64.8 1.9 %results.1 = (bf16[192,512]{1,0:T(8,128)(2,1)}, bf16[192,256]{1,0:T(8,128)(2,1)}, bf16[192,256]{1,0:T(8,128)(2,1)}, bf16[192,256]{1,0:T(8,128)(2,1)}, bf16[256,128]{1,0:T(8,128)(2,1)}) custom-call(bf16[192,512]{1,0:T(8,128)(2,1)} %get-tuple-element.10.refs_0_, bf16[192,256]{1,0:T(8,128)(2,1)} %get-tuple-element.11.refs_1_, ...), custom_call_target="tpu_custom_call" | custom-call | tf_op jit(solution)/shard_map/results/pallas_call | solution.py:560
